TPU v7x, 512 devices: a whole 4x8x8 slice. The times are simulated.
512 devices in a mesh: enc: 128 (over x, y_hi, z), dec: 4 (over y_lo, core).
Axes of the slice: x: 4, y: 8 (y_hi: 4, y_lo: 2; y = y_hi * 2 + y_lo), z: 8, core: 2. Of those that a mesh axis runs over, the one named last changes fastest.
Arguments:
- dec_states: bfloat16 [2, 8192, 2048], P(None, 'enc'), may hold values from -24 to 24
- enc_states: bfloat16 [2, 32768, 2048], P(None, 'enc'), may hold values from -144 to 144
- w_query: bfloat16 [2048, 2048], P('enc', 'dec'), may hold values from -0.125 to 0.125
- w_key: bfloat16 [2048, 2048], P('enc', 'dec'), may hold values from -0.125 to 0.125
- w_value: bfloat16 [2048, 2048], P('enc', 'dec'), may hold values from -0.125 to 0.125
- passage_slot: int32 [128, 4], P('enc'), may hold values from 0 to 3, each once within a row
- ctx_grad: bfloat16 [2, 8192, 2048], P(None, 'enc', 'dec'), may hold values from -24 to 24
Outputs:
- context: bfloat16 [2, 8192, 2048], P(None, 'enc', 'dec')
- grad_query: float32 [2048, 2048], P('enc', 'dec')
- grad_enc: bfloat16 [2, 32768, 2048], P(None, 'enc')
All inputs are finite; a program needn't handle non-finite values.
Results may differ from a plain program's by a relative error of at most 0.022.
The roundings to bfloat16 on the way count: a program that leaves them out, or rounds other values in their place, can miss the bound.
Values may be sent and summed in bfloat16 or wider, within the bound.
No kernel may reach another device: no remote copies, remote signals or barrier semaphores. Data moves between devices by JAX's collectives and lax.ppermute only.
A program may use at most 64 MiB of HBM per device.

v0:
```python
import jax
import jax.numpy as jnp
from jax import lax
from jax.sharding import PartitionSpec as P

HEAD_DIM = 64


SCALE = 0.125


def passed_along(x, axis, by):
    size = lax.axis_size(axis)
    return lax.ppermute(x, axis, [(i, (i + by) % size) for i in range(size)])


def question_pass(queries, key_rows, value_rows, grad_out, head_count):
    query_count = queries.shape[0]
    key_count = key_rows.shape[0]
    query_heads = queries.reshape(query_count, head_count, HEAD_DIM)
    key_heads = key_rows.reshape(key_count, head_count, HEAD_DIM)
    value_heads = value_rows.reshape(key_count, head_count, HEAD_DIM)
    grad_heads = grad_out.reshape(query_count, head_count, HEAD_DIM)
    scores = (
        jnp.einsum("qhd,khd->hqk", query_heads, key_heads, preferred_element_type=jnp.float32)
        * SCALE
    )
    largest = jnp.max(scores, axis=-1, keepdims=True)
    raw_weights = jnp.exp(scores - largest)
    attention = raw_weights / jnp.sum(raw_weights, axis=-1, keepdims=True)
    attention_low = attention.astype(jnp.bfloat16)
    context = jnp.einsum(
        "hqk,khd->qhd", attention_low, value_heads, preferred_element_type=jnp.float32
    ).astype(jnp.bfloat16)
    grad_attention = jnp.einsum(
        "qhd,khd->hqk", grad_heads, value_heads, preferred_element_type=jnp.float32
    )
    correction = jnp.sum(attention * grad_attention, axis=-1, keepdims=True)
    grad_scores = (attention * (grad_attention - correction) * SCALE).astype(jnp.bfloat16)
    grad_values = jnp.einsum(
        "hqk,qhd->khd", attention_low, grad_heads, preferred_element_type=jnp.float32
    ).astype(jnp.bfloat16)
    grad_keys = jnp.einsum(
        "hqk,qhd->khd", grad_scores, query_heads, preferred_element_type=jnp.float32
    ).astype(jnp.bfloat16)
    grad_queries = jnp.einsum(
        "hqk,khd->qhd", grad_scores, key_heads, preferred_element_type=jnp.float32
    ).astype(jnp.bfloat16)
    inner_width = head_count * HEAD_DIM
    return (
        context.reshape(query_count, inner_width),
        grad_queries.reshape(query_count, inner_width),
        grad_keys.reshape(key_count, inner_width),
        grad_values.reshape(key_count, inner_width),
    )


def on_device(dec_states, enc_states, w_query, w_key, w_value, passage_slot, ctx_grad):
    batches, dec_rows, model_width = dec_states.shape
    enc_rows = enc_states.shape[1]
    inner_width = w_query.shape[1]
    head_count = inner_width // HEAD_DIM
    passage_count = passage_slot.shape[1]
    passage_len = enc_rows // passage_count
    dec_flat = dec_states.reshape(batches * dec_rows, model_width)
    enc_flat = enc_states.reshape(batches * enc_rows, model_width)
    columns = dec_flat
    queries = jnp.dot(
        columns,
        lax.all_gather(w_query, "enc", axis=0, tiled=True),
        preferred_element_type=jnp.float32,
    )
    key_full, value_full = (
        lax.all_gather(w_key, "enc", axis=0, tiled=True),
        lax.all_gather(w_value, "enc", axis=0, tiled=True),
    )
    queries = queries.astype(jnp.bfloat16).reshape(batches, dec_rows, inner_width)
    key_local = jnp.dot(enc_flat, key_full, preferred_element_type=jnp.float32).astype(jnp.bfloat16)
    value_local = jnp.dot(enc_flat, value_full, preferred_element_type=jnp.float32).astype(
        jnp.bfloat16
    )
    local_pair = jnp.stack((key_local, value_local)).reshape(
        2, batches, passage_count, passage_len, inner_width
    )
    order = passage_slot[0]
    outgoing = [
        lax.dynamic_index_in_dim(local_pair, order[offset], 2, False)
        for offset in range(passage_count)
    ]
    arrived = [outgoing[0]] + [
        passed_along(outgoing[offset], "enc", -offset) for offset in range(1, passage_count)
    ]
    gathered = jnp.concatenate(arrived, axis=2)
    contexts = []
    query_grads = []
    key_grads = []
    value_grads = []
    for micro_batch in range(batches):
        results = question_pass(
            queries[micro_batch],
            gathered[0, micro_batch],
            gathered[1, micro_batch],
            ctx_grad[micro_batch],
            head_count,
        )
        contexts.append(results[0])
        query_grads.append(results[1])
        key_grads.append(results[2])
        value_grads.append(results[3])
    context = jnp.stack(contexts)
    query_grad_all = jnp.stack(query_grads).reshape(batches * dec_rows, inner_width)
    returning = jnp.stack((jnp.stack(key_grads), jnp.stack(value_grads))).reshape(
        2, batches, passage_count, passage_len, inner_width
    )
    outgoing_grads = [returning[:, :, offset] for offset in range(passage_count)]
    returned = [outgoing_grads[0]] + [
        passed_along(outgoing_grads[offset], "enc", offset) for offset in range(1, passage_count)
    ]
    by_offset = jnp.stack(returned)
    positions = jnp.arange(passage_count, dtype=jnp.int32)
    inverse = jnp.sum(
        positions[:, None] * (order[:, None] == positions[None, :]).astype(jnp.int32), axis=0
    )
    by_slot = jnp.take(by_offset, inverse, axis=0)
    by_slot = jnp.transpose(by_slot, (1, 2, 0, 3, 4)).reshape(2, batches * enc_rows, inner_width)
    partial_value = jnp.einsum(
        "ri,di->rd", by_slot[0], key_full, preferred_element_type=jnp.float32
    )
    partial_value = partial_value + jnp.einsum(
        "ri,di->rd", by_slot[1], value_full, preferred_element_type=jnp.float32
    )
    rounded = lax.optimization_barrier(partial_value.astype(jnp.bfloat16))
    summed = lax.psum(rounded.astype(jnp.float32).astype(jnp.bfloat16), "dec")
    grad_enc = summed.reshape(batches, enc_rows, model_width)
    columns = dec_flat
    grad_query = lax.psum_scatter(
        lax.dot_general(
            columns, query_grad_all, (((0,), (0,)), ((), ())), preferred_element_type=jnp.float32
        ),
        "enc",
        scatter_dimension=0,
        tiled=True,
    )
    return (context, grad_query, grad_enc)


def solution(mesh):
    in_specs = (
        P(None, "enc", None),
        P(None, "enc", None),
        P("enc", "dec"),
        P("enc", "dec"),
        P("enc", "dec"),
        P("enc", None),
        P(None, "enc", "dec"),
    )
    out_specs = (P(None, "enc", "dec"), P("enc", "dec"), P(None, "enc", None))
    return jax.shard_map(
        on_device, mesh=mesh, in_specs=in_specs, out_specs=out_specs, check_vma=False
    )
```

profile of v0, /device:TPU:8, one launch (start us, length us, event | category | flops | bytes accessed | tf_op | source)
XLA Modules:
  0.0 1329.4 jit_solution(8756275389959634545)
XLA Ops:
  9.4 1.4 fusion.65
  22.3 117.6 %all-gather.6.cloned.1.call-done = bf16[2048,512]{1,0:T(8,128)(2,1)} async-done(((bf16[16,512]{1,0:T(8,128)(2,1)}), bf16[2048,512]{1,0:T(8,128)(2,1)}) %all-gather.6.cloned.1.call-update) | async-done | bytes 2097168 | tf_op jit(solution)/shard_map/all_gather | solution.py:75
  139.9 2.8 convolution_convert_fusion
  142.8 121.8 %all-gather.4.cloned.1.call-done = bf16[2048,512]{1,0:T(8,128)(2,1)} async-done(((bf16[16,512]{1,0:T(8,128)(2,1)}), bf16[2048,512]{1,0:T(8,128)(2,1)}) %all-gather.4.cloned.1.call-update) | async-done | bytes 2097168 | tf_op jit(solution)/shard_map/all_gather | solution.py:74
  264.5 2.8 convolution_convert_fusion.1
  268.3 8.4 collective-permute-start
  276.7 2.8 collective-permute-start.1
  279.6 4.7 collective-permute-start.2
  284.3 118.7 %all-gather.8.cloned.1.call-done = bf16[2048,512]{1,0:T(8,128)(2,1)} async-done(((bf16[16,512]{1,0:T(8,128)(2,1)}), bf16[2048,512]{1,0:T(8,128)(2,1)}) %all-gather.8.cloned.1.call-update) | async-done | bytes 2097168 | tf_op jit(solution)/shard_map/all_gather | solution.py:70
  403.0 2.0 convolution_convert_fusion.10
  407.6 2.1 convolution_bitcast_fusion.1
  409.7 2.1 fusion.66
  411.8 2.3 fusion.19
  415.6 4.8 fusion.17
  422.7 2.0 convolution_bitcast_fusion.2
  425.9 1.5 fusion.18
  428.6 4.9 fusion.16
  437.0 3.6 collective-permute-start.4
  440.6 3.9 collective-permute-start.5
  444.5 3.2 collective-permute-start.3
  447.8 19.8 %collective-permute-done.4 = bf16[2,2,64,512]{3,2,1,0:T(8,128)(2,1)S(1)} collective-permute-done((bf16[2,2,64,512]{3,2,1,0:T(8,128)(2,1)S(1)}, bf16[2,2,64,512]{3,2,1,0:T(8,128)(2,1)S(1)}, u32[]{:S(2)}, u32[]{:S(2)}) %collective-permute-start.4) | collective-permute-done | bytes 262176 | tf_op jit(solution)/shard_map/ppermute | solution.py:14
  467.6 12.0 collective-permute-done.3
  480.8 1.8 gather_fusion
  483.0 1.4 copy-done.4
  486.0 2.6 add_convert_fusion
  489.5 4.0 convolution_convert_fusion.6
  493.7 4.1 convolution_convert_fusion.7
  497.9 2.7 convolution_bitcast_fusion
  500.6 5.4 copy.110
  509.3 41.1 %all-reduce.2.cloned.1.call-done = bf16[2,256,2048]{2,1,0:T(8,128)(2,1)} async-done(((bf16[2,256,2048]{2,1,0:T(8,128)(2,1)}), bf16[2,256,2048]{2,1,0:T(8,128)(2,1)}) %all-reduce.2.cloned.1.call-update) | async-done | bytes 2097168 | tf_op jit(solution)/shard_map/psum | solution.py:133
  550.4 769.3 %reduce-scatter.4.cloned.1.call-done = f32[16,512]{1,0:T(8,128)} async-done(((f32[2048,512]{1,0:T(8,128)}), f32[16,512]{1,0:T(8,128)}) %reduce-scatter.4.cloned.1.call-update) | async-done | bytes 32784
  1319.7 3.2 copy.123
  (84 shorter events, 26.5 us)
Async XLA Ops:
  7.2 132.8 %copy-start = (bf16[2,256,2048]{2,1,0:T(8,128)(2,1)S(1)}, bf16[2,256,2048]{2,1,0:T(8,128)(2,1)}, u32[]{:S(2)}) copy-start(bf16[2,256,2048]{2,1,0:T(8,128)(2,1)} %param.8) | copy-start | bytes 6291460
  7.2 132.7 %all-gather.6.cloned.1.call-start = ((), (), s32[]{:S(2)}) async-start(), calls=%async_computation.2 | async-start | bytes 2113536 | tf_op jit(solution)/shard_map/all_gather | solution.py:75
  7.9 256.6 %all-gather.4.cloned.1.call-start = ((), (), s32[]{:S(2)}) async-start(), calls=%async_computation.1 | async-start | bytes 2113536 | tf_op jit(solution)/shard_map/all_gather | solution.py:74
  8.7 394.3 %all-gather.8.cloned.1.call-start = ((), (), s32[]{:S(2)}) async-start(), calls=%async_computation.3 | async-start | bytes 2113536 | tf_op jit(solution)/shard_map/all_gather | solution.py:70
  9.4 541.0 %all-reduce.2.cloned.1.call-start = ((), (), s32[]{:S(2)}) async-start(), calls=%async_computation.4 | async-start | bytes 4194304 | tf_op jit(solution)/shard_map/psum | solution.py:133
  21.8 0.5 copy-start.13
  267.4 135.6 %copy-start.2 = (bf16[2,64,2048]{2,1,0:T(8,128)(2,1)S(1)}, bf16[2,64,2048]{2,1,0:T(8,128)(2,1)}, u32[]{:S(2)}) copy-start(bf16[2,64,2048]{2,1,0:T(8,128)(2,1)} %param.7) | copy-start | bytes 1572868
  268.3 137.7 %collective-permute-start = (bf16[2,2,64,512]{3,2,1,0:T(8,128)(2,1)}, bf16[2,2,64,512]{3,2,1,0:T(8,128)(2,1)S(1)}, u32[]{:S(2)}, u32[]{:S(2)}) collective-permute-start(bf16[2,2,64,512]{3,2,1,0:T(8,128)(2,1)} %get-tuple-element.26), channel_id=1, source_target_pairs={{0,508},{4,0},{8,4},{12,8},{16,12},{20,16},{24,20},{28,24},{32,28}... | collective-permute-start | bytes 786440 | tf_op jit(solution)/shard_map/ppermute | solution.py:14
  276.7 129.2 %collective-permute-start.1 = (bf16[2,2,64,512]{3,2,1,0:T(8,128)(2,1)}, bf16[2,2,64,512]{3,2,1,0:T(8,128)(2,1)S(1)}, u32[]{:S(2)}, u32[]{:S(2)}) collective-permute-start(bf16[2,2,64,512]{3,2,1,0:T(8,128)(2,1)} %get-tuple-element.27), channel_id=1, source_target_pairs={{0,504},{4,508},{8,0},{12,4},{16,8},{20,12},{24,16},{28,20},{32,24... | collective-permute-start | bytes 786440 | tf_op jit(solution)/shard_map/ppermute | solution.py:14
  279.6 126.4 %collective-permute-start.2 = (bf16[2,2,64,512]{3,2,1,0:T(8,128)(2,1)}, bf16[2,2,64,512]{3,2,1,0:T(8,128)(2,1)}, u32[]{:S(2)}, u32[]{:S(2)}) collective-permute-start(bf16[2,2,64,512]{3,2,1,0:T(8,128)(2,1)} %get-tuple-element.28), channel_id=1, source_target_pairs={{0,500},{4,504},{8,508},{12,0},{16,4},{20,8},{24,12},{28,16},{32,2... | collective-permute-start | bytes 786440 | tf_op jit(solution)/shard_map/ppermute | solution.py:14
  407.3 6.7 copy-start.7
  407.5 4.3 copy-start.9
  407.6 15.1 %copy-start.5 = (bf16[1,1,256,512]{2,3,1,0:T(8,128)(2,1)}, bf16[1,1,256,512]{2,3,1,0:T(8,128)(2,1)S(1)}, u32[]{:S(2)}) copy-start(bf16[1,1,256,512]{2,3,1,0:T(8,128)(2,1)S(1)} %copy.80) | copy-start | bytes 786436
  428.6 7.1 copy-start.11
  435.8 12.0 copy-start.14
  437.0 30.6 %collective-permute-start.4 = (bf16[2,2,64,512]{3,2,1,0:T(8,128)(2,1)S(1)}, bf16[2,2,64,512]{3,2,1,0:T(8,128)(2,1)S(1)}, u32[]{:S(2)}, u32[]{:S(2)}) collective-permute-start(bf16[2,2,64,512]{3,2,1,0:T(8,128)(2,1)S(1)} %get-tuple-element.18), channel_id=1, source_target_pairs={{0,8},{4,12},{8,16},{12,20},{16,24},{20,28},{24,32},{28,36},{32,40... | collective-permute-start | bytes 786440 | tf_op jit(solution)/shard_map/ppermute | solution.py:14
  440.6 27.0 %collective-permute-start.5 = (bf16[2,2,64,512]{3,2,1,0:T(8,128)(2,1)S(1)}, bf16[2,2,64,512]{3,2,1,0:T(8,128)(2,1)S(1)}, u32[]{:S(2)}, u32[]{:S(2)}) collective-permute-start(bf16[2,2,64,512]{3,2,1,0:T(8,128)(2,1)S(1)} %get-tuple-element.19), channel_id=1, source_target_pairs={{0,12},{4,16},{8,20},{12,24},{16,28},{20,32},{24,36},{28,40},{32,4... | collective-permute-start | bytes 786440 | tf_op jit(solution)/shard_map/ppermute | solution.py:14
  444.5 35.1 %collective-permute-start.3 = (bf16[2,2,64,512]{3,2,1,0:T(8,128)(2,1)S(1)}, bf16[2,2,64,512]{3,2,1,0:T(8,128)(2,1)S(1)}, u32[]{:S(2)}, u32[]{:S(2)}) collective-permute-start(bf16[2,2,64,512]{3,2,1,0:T(8,128)(2,1)S(1)} %get-tuple-element.20), channel_id=1, source_target_pairs={{0,4},{4,8},{8,12},{12,16},{16,20},{20,24},{24,28},{28,32},{32,36}... | collective-permute-start | bytes 786440 | tf_op jit(solution)/shard_map/ppermute | solution.py:14
  482.8 1.6 copy-start.4
  484.4 1.6 copy-start.1
  488.6 0.9 copy-start.8
  488.6 831.1 %reduce-scatter.4.cloned.1.call-start = ((), (), s32[]{:S(2)}) async-start(), calls=%async_computation.5 | async-start | bytes 4227072
  493.5 4.3 copy-start.3
  506.0 1.0 copy-start.10
  506.0 1.0 copy-start.12
  506.9 0.9 copy-start.6
Sparse Core Ops, SparseCore 0:
  12.6 127.2 all-gather.5
  144.5 119.9 all-gather.3
  269.1 133.8 all-gather.7
  488.7 61.6 all-reduce.1
  553.8 765.8 reduce-scatter.3
where the time goes:
time: 1330 us
  waiting for transfers between devices  1200 us (90%)
  matrix products  44.3 us (3%)
  local copies, waits for them, and re-layouts  27.8 us (2%)
  starting transfers between devices  27 us (2%)
  between operations  21.9 us (2%)
    unnamed x6, waiting for transfers between devices  771 us
    all_gather x1, waiting for transfers between devices, on_device(): lax.all_gather(w_key, 'enc', axis=0, tiled=True)  122 us
    all_gather x1, waiting for transfers between devices, on_device(): lax.all_gather(w_query, 'enc', axis=0, tiled=True)  119 us
    all_gather x1, waiting for transfers between devices, on_device(): lax.all_gather(w_value, 'enc', axis=0, tiled=True)  118 us
    psum x1, waiting for transfers between devices, on_device(): summed = lax.psum(rounded.astype(jnp.float32).astype(jnp.bfloat16), 'dec')  41.1 us
    ppermute x6, waiting for transfers between devices, passed_along(): return lax.ppermute(x, axis, [(i, (i + by) % size) for i in range(size)])  31.9 us
    ppermute x6, starting transfers between devices, passed_along(): return lax.ppermute(x, axis, [(i, (i + by) % size) for i in range(size)])  26.6 us
  transfers between devices with their start and end apart: 11, of which 7 were waited for; matrix products, arithmetic and copies ran while one was open for 2% of the time, Pallas kernels for 0%

commit v1 on v0

v1 whole, which is shorter than its diff:
```python
import jax
import jax.numpy as jnp
from jax import lax
from jax.experimental import pallas as pl
from jax.experimental.pallas import tpu as pltpu
from jax.sharding import Mesh, PartitionSpec as P

HEAD_DIM = 64
SCALE = 0.125
LOW = jnp.bfloat16
WIDE = jnp.float32
AXES = ("x", "yh", "z", "yl", "core")
SIZES = (4, 4, 8, 2, 2)
ENC = ("x", "yh", "z")
PLANE = ("yh", "z")
DEC = ("yl", "core")
GROUP = 256


def exchange(x, axis):
    return lax.all_to_all(x, axis, split_axis=0, concat_axis=0, tiled=True)


def spread(x, axis, size):
    return exchange(jnp.broadcast_to(x[None], (size,) + x.shape), axis)


def passed_along(x, by):
    size = SIZES[0] * SIZES[1] * SIZES[2]
    return lax.ppermute(x, ENC, [(i, (i + by) % size) for i in range(size)])


def dot(a, b, contract):
    return lax.dot_general(a, b, ((contract[:1], contract[1:]), ((), ())), preferred_element_type=WIDE)


def attention_kernel(q_ref, kv_ref, grad_ref, ctx_ref, gq_ref, gkv_ref):
    rows, width = q_ref.shape
    batches = 2
    queries = rows // batches
    keys = kv_ref.shape[0] // batches
    heads = GROUP // HEAD_DIM
    row_head = lax.broadcasted_iota(jnp.int32, (heads * queries, GROUP), 0) // queries
    col_head = lax.broadcasted_iota(jnp.int32, (heads * queries, GROUP), 1) // HEAD_DIM
    own = row_head == col_head
    col_small = lax.broadcasted_iota(jnp.int32, (queries, GROUP), 1) // HEAD_DIM

    def per_head(x):
        return jnp.where(own, jnp.concatenate([x] * heads, axis=0), jnp.zeros((), x.dtype))

    def merged(x):
        out = x[:queries]
        for h in range(1, heads):
            out = jnp.where(col_small == h, x[h * queries : (h + 1) * queries], out)
        return out

    for b in range(batches):
        for g in range(width // GROUP):
            qs, ks = pl.ds(b * queries, queries), pl.ds(b * keys, keys)
            cs, vs = pl.ds(g * GROUP, GROUP), pl.ds(width + g * GROUP, GROUP)
            query = per_head(q_ref[qs, cs])
            grad = per_head(grad_ref[qs, cs])
            key, value = kv_ref[ks, cs], kv_ref[ks, vs]
            scores = dot(query, key, (1, 1)) * SCALE
            raw = jnp.exp(scores - jnp.max(scores, axis=-1, keepdims=True))
            attention = raw / jnp.sum(raw, axis=-1, keepdims=True)
            low = attention.astype(LOW)
            ctx_ref[qs, cs] = merged(dot(low, value, (1, 0))).astype(LOW)
            grad_attention = dot(grad, value, (1, 1))
            correction = jnp.sum(attention * grad_attention, axis=-1, keepdims=True)
            grad_scores = (attention * (grad_attention - correction) * SCALE).astype(LOW)
            gkv_ref[ks, vs] = dot(low, grad, (0, 0)).astype(LOW)
            gkv_ref[ks, cs] = dot(grad_scores, query, (0, 0)).astype(LOW)
            gq_ref[qs, cs] = merged(dot(grad_scores, key, (1, 0))).astype(LOW)


def attention_pass(q, kv, grad):
    whole = pl.BlockSpec(memory_space=pltpu.VMEM)
    return pl.pallas_call(
        attention_kernel,
        out_shape=(
            jax.ShapeDtypeStruct(q.shape, LOW),
            jax.ShapeDtypeStruct(q.shape, LOW),
            jax.ShapeDtypeStruct(kv.shape, LOW),
        ),
        in_specs=[whole] * 3,
        out_specs=(whole,) * 3,
        compiler_params=pltpu.CompilerParams(vmem_limit_bytes=24 * 1024 * 1024),
        cost_estimate=pl.CostEstimate(flops=940_000_000, bytes_accessed=3 << 20, transcendentals=1 << 18),
    )(q, kv, grad)


def on_device(dec_states, enc_states, w_query, w_key, w_value, passage_slot, ctx_grad):
    batches, dec_rows, model = dec_states.shape
    enc_rows = enc_states.shape[1]
    width = w_query.shape[1]
    passages = passage_slot.shape[1]
    length = enc_rows // passages
    half = length // 2
    quarter = model // 4
    dec_flat = dec_states.reshape(batches * dec_rows, model)
    yl, core = lax.axis_index("yl"), lax.axis_index("core")
    order = passage_slot[0]
    positions = jnp.arange(passages, dtype=jnp.int32)
    inverse = jnp.sum(positions[:, None] * (order[:, None] == positions[None, :]).astype(jnp.int32), axis=0)

    by_slot = enc_states.reshape(batches, passages, length, model)
    own_part = lax.dynamic_index_in_dim(by_slot, core, 0, False)
    own_part = lax.dynamic_slice_in_dim(own_part, yl * half, half, 1)
    parts = jnp.stack(
        [passed_along(lax.dynamic_index_in_dim(own_part, order[j], 0, False), -j) for j in range(1, passages)]
    )
    parts = lax.all_gather(parts, DEC, axis=0, tiled=False)
    parts = parts.reshape(2, 2, passages - 1, half, model)
    parts = jnp.transpose(parts, (1, 2, 0, 3, 4)).reshape(batches, passages - 1, length, model)
    near = lax.dynamic_index_in_dim(by_slot, order[0], 1, True)
    enc_flat = jnp.concatenate([near, parts], axis=1).reshape(batches * enc_rows, model)

    weights = spread(jnp.concatenate([w_key, w_value, w_query], axis=1), PLANE, 32).reshape(quarter, 3 * width)
    weight_kv = spread(weights[:, : 2 * width], "x", 4).reshape(model, 2 * width)
    weight_q = weights[:, 2 * width :]

    dec_quarter = dec_flat.reshape(batches * dec_rows, 4, quarter)
    dec_quarter = exchange(jnp.transpose(dec_quarter, (1, 0, 2)), "x").reshape(4 * batches * dec_rows, quarter)
    q_parts = dot(dec_quarter, weight_q, (1, 0)).reshape(4, batches * dec_rows, width)
    queries = jnp.sum(exchange(q_parts, "x"), axis=0).astype(LOW)

    kv = dot(enc_flat, weight_kv, (1, 0)).astype(LOW)
    context, grad_queries, grad_kv = attention_pass(queries, kv, ctx_grad.reshape(batches * dec_rows, width))

    partial = dot(grad_kv, weight_kv, (1, 1)).astype(LOW).reshape(batches, passages, 2, half, model)
    partial = jnp.transpose(partial, (2, 0, 1, 3, 4)).reshape(4, passages, half, model)
    received = exchange(partial, DEC)
    summed = jnp.sum(received.astype(WIDE), axis=0).astype(LOW)
    back = jnp.stack([summed[0]] + [passed_along(summed[j], j) for j in range(1, passages)])
    back = jnp.take(back, inverse, axis=0)
    back = lax.all_gather(back, DEC, axis=0, tiled=False).reshape(2, 2, passages, half, model)
    grad_enc = jnp.transpose(back, (1, 2, 0, 3, 4)).reshape(batches, enc_rows, model)

    gq = spread(grad_queries, "x", 4).reshape(4 * batches * dec_rows, width)
    share = dot(dec_quarter, gq, (0, 0)).astype(LOW).reshape(32, quarter // 32, width)
    grad_query = jnp.sum(exchange(share, PLANE).astype(WIDE), axis=0)
    return context.reshape(batches, dec_rows, width), grad_query, grad_enc


def solution(mesh):
    fine = Mesh(mesh.devices.reshape(SIZES), AXES)
    in_specs = (
        P(None, ENC, None),
        P(None, ENC, None),
        P(ENC, DEC),
        P(ENC, DEC),
        P(ENC, DEC),
        P(ENC, None),
        P(None, ENC, DEC),
    )
    out_specs = (P(None, ENC, DEC), P(ENC, DEC), P(None, ENC, None))
    return jax.shard_map(on_device, mesh=fine, in_specs=in_specs, out_specs=out_specs, check_vma=False)
```

time: 1330 us -> 291 us (0.22)
  the two profiles are of different devices: /device:TPU:8 before, /device:TPU:1 now
where the time goes in v1:
time: 291 us; the launch traced here: 290 us
  waiting for transfers between devices  128 us (44%)
  starting transfers between devices  62.2 us (21%)
  blocking collectives  41.9 us (14%)
  between operations  22 us (8%)
  local copies, waits for them, and re-layouts  16.6 us (6%)
  matrix products  11 us (4%)
  other arithmetic  4.53 us (2%)
  Pallas kernels  3.1 us (1%)
    all_to_all x5, waiting for transfers between devices, exchange(): return lax.all_to_all(x, axis, split_axis=0, concat_axis=0, tiled=True)  81.5 us
    all_to_all x2, blocking collectives, exchange(): return lax.all_to_all(x, axis, split_axis=0, concat_axis=0, tiled=True)  41.9 us
    all_to_all x5, starting transfers between devices, exchange(): return lax.all_to_all(x, axis, split_axis=0, concat_axis=0, tiled=True)  34.7 us
    ppermute x6, starting transfers between devices, passed_along(): return lax.ppermute(x, ENC, [(i, (i + by) % size) for i in range(size)])  27.4 us
    ppermute x6, waiting for transfers between devices, passed_along(): return lax.ppermute(x, ENC, [(i, (i + by) % size) for i in range(size)])  24.3 us
    all_gather x1, waiting for transfers between devices, on_device(): parts = lax.all_gather(parts, DEC, axis=0, tiled=False)  22.4 us
    dot_general x4, matrix products, dot(): lax.dot_general(a, b, ((contract[:1], contract[1:]), ((), ())), preferred...  11 us
  transfers between devices with their start and end apart: 13, of which 10 were waited for; matrix products, arithmetic and copies ran while one was open for 3% of the time, Pallas kernels for 0%

profile of v1, /device:TPU:1, one launch (start us, length us, event | category | flops | bytes accessed | tf_op | source)
XLA Modules:
  0.0 289.5 jit_solution(18221159653442643288)
XLA Ops:
  7.2 1.4 reshape_reshape.3
  9.8 4.8 %all-to-all-start.1 = ((bf16[4,128,512]{1,2,0:T(8,128)(2,1)}), bf16[4,128,512]{1,2,0:T(8,128)(2,1)S(1)}, u32[]{:S(2)}, u32[]{:S(2)}) async-start(bf16[4,128,512]{1,2,0:T(8,128)(2,1)} %bitcast.1), calls=%async_computation.1 | async-start | bytes 1048576 | tf_op jit(solution)/shard_map/all_to_all | solution.py:21
  14.7 6.9 %all-to-all-done.1 = bf16[4,128,512]{1,2,0:T(8,128)(2,1)S(1)} async-done(((bf16[4,128,512]{1,2,0:T(8,128)(2,1)}), bf16[4,128,512]{1,2,0:T(8,128)(2,1)S(1)}, u32[]{:S(2)}, u32[]{:S(2)}) %all-to-all-start.1) | async-done | bytes 524320 | tf_op jit(solution)/shard_map/all_to_all | solution.py:21
  22.9 17.0 %all-to-all-start = ((bf16[32,16,1536]{2,1,0:T(8,128)(2,1)}), bf16[32,16,1536]{2,1,0:T(8,128)(2,1)S(1)}, u32[]{:S(2)}, u32[]{:S(2)}) async-start(bf16[32,16,1536]{2,1,0:T(8,128)(2,1)} %broadcast_in_dim.16), calls=%async_computation | async-start | bytes 3145728 | tf_op jit(solution)/shard_map/all_to_all | solution.py:21
  40.2 42.1 %all-to-all-done = bf16[32,16,1536]{2,1,0:T(8,128)(2,1)S(1)} async-done(((bf16[32,16,1536]{2,1,0:T(8,128)(2,1)}), bf16[32,16,1536]{2,1,0:T(8,128)(2,1)S(1)}, u32[]{:S(2)}, u32[]{:S(2)}) %all-to-all-start) | async-done | bytes 1572896 | tf_op jit(solution)/shard_map/all_to_all | solution.py:21
  82.3 1.4 fusion.1
  83.7 4.2 %all-to-all-start.2 = ((f32[4,128,512]{2,1,0:T(8,128)}), f32[4,128,512]{2,1,0:T(8,128)}, u32[]{:S(2)}, u32[]{:S(2)}) async-start(f32[4,128,512]{2,1,0:T(8,128)} %bitcast.4), calls=%async_computation.2 | async-start | bytes 2097152 | tf_op jit(solution)/shard_map/all_to_all | solution.py:21
  94.5 7.7 %all-to-all-done.2 = f32[4,128,512]{2,1,0:T(8,128)} async-done(((f32[4,128,512]{2,1,0:T(8,128)}), f32[4,128,512]{2,1,0:T(8,128)}, u32[]{:S(2)}, u32[]{:S(2)}) %all-to-all-start.2) | async-done | bytes 1048608 | tf_op jit(solution)/shard_map/all_to_all | solution.py:21
  102.3 2.5 broadcast_in_dim.17
  104.8 4.8 %all-to-all-start.3 = ((bf16[4,512,1024]{2,1,0:T(8,128)(2,1)}), bf16[4,512,1024]{2,1,0:T(8,128)(2,1)}, u32[]{:S(2)}, u32[]{:S(2)}) async-start(bf16[4,512,1024]{2,1,0:T(8,128)(2,1)} %broadcast_in_dim.17), calls=%async_computation.3 | async-start | bytes 8388608 | tf_op jit(solution)/shard_map/all_to_all | solution.py:21
  110.9 4.2 %collective-permute-start.2 = (bf16[32,2048]{1,0:T(8,128)(2,1)S(1)}, bf16[32,2048]{1,0:T(8,128)(2,1)S(1)}, u32[]{:S(2)}, u32[]{:S(2)}) collective-permute-start(bf16[32,2048]{1,0:T(8,128)(2,1)S(1)} %get-tuple-element.10), channel_id=1, source_target_pairs={{0,500},{4,504},{8,508},{12,0},{16,4},{20,8},{24,12},{28,16},{32,2... | collective-permute-start | bytes 393224 | tf_op jit(solution)/shard_map/ppermute | solution.py:30
  115.1 1.9 collective-permute-start.1
  117.0 8.8 %collective-permute-start = (bf16[32,2048]{1,0:T(8,128)(2,1)S(1)}, bf16[32,2048]{1,0:T(8,128)(2,1)S(1)}, u32[]{:S(2)}, u32[]{:S(2)}) collective-permute-start(bf16[32,2048]{1,0:T(8,128)(2,1)S(1)} %get-tuple-element.9), channel_id=1, source_target_pairs={{0,508},{4,0},{8,4},{12,8},{16,12},{20,16},{24,20},{28,24},{32,28}... | collective-permute-start | bytes 393224 | tf_op jit(solution)/shard_map/ppermute | solution.py:30
  125.9 5.2 %collective-permute-done.1 = bf16[32,2048]{1,0:T(8,128)(2,1)S(1)} collective-permute-done((bf16[32,2048]{1,0:T(8,128)(2,1)S(1)}, bf16[32,2048]{1,0:T(8,128)(2,1)S(1)}, u32[]{:S(2)}, u32[]{:S(2)}) %collective-permute-start.1) | collective-permute-done | bytes 131104 | tf_op jit(solution)/shard_map/ppermute | solution.py:30
  131.1 3.0 %collective-permute-done = bf16[32,2048]{1,0:T(8,128)(2,1)S(1)} collective-permute-done((bf16[32,2048]{1,0:T(8,128)(2,1)S(1)}, bf16[32,2048]{1,0:T(8,128)(2,1)S(1)}, u32[]{:S(2)}, u32[]{:S(2)}) %collective-permute-start) | collective-permute-done | bytes 131104 | tf_op jit(solution)/shard_map/ppermute | solution.py:30
  138.0 22.4 %all-gather.6.cloned.1.call-done = bf16[12,32,2048]{2,1,0:T(8,128)(2,1)} async-done(((bf16[3,32,2048]{2,1,0:T(8,128)(2,1)}), bf16[12,32,2048]{2,1,0:T(8,128)(2,1)}) %all-gather.6.cloned.1.call-update) | async-done | bytes 1572880 | tf_op jit(solution)/shard_map/all_gather | solution.py:113
  160.4 1.5 copy.26
  163.5 4.6 %convolution_convert_fusion.1.kv_ref = bf16[512,1024]{1,0:T(8,128)(2,1)S(1)} fusion(bf16[512,2048]{1,0:T(8,128)(2,1)S(1)} %bitcast.74, bf16[2048,1024]{1,0:T(8,128)(2,1)} %bitcast.20), kind=kOutput, calls=%fused_computation.3 | convolution fusion | flops 2148007936 | bytes 7340032 | tf_op jit(solution)/shard_map/dot_general | solution.py:34
  168.0 3.1 %shard_map.94 = (bf16[128,512]{1,0:T(8,128)(2,1)}, bf16[128,512]{1,0:T(8,128)(2,1)S(1)}, bf16[512,1024]{1,0:T(8,128)(2,1)S(1)}) custom-call(bf16[128,512]{1,0:T(8,128)(2,1)S(1)} %reduce_sum.41.q_ref, bf16[512,1024]{1,0:T(8,128)(2,1)S(1)} %convolution_convert_fusion.1.kv_ref, bf16[128,512]{1,0:T(8,128)(2,1)S(1)} %bitcast.66), custom_call_target="tpu_custom_call" | custom-call | flops 940000000 | bytes 3145728 | tf_op jit(solution)/shard_map/pallas_call | solution.py:79
  171.1 4.6 %convolution_convert_fusion = bf16[512,2048]{1,0:T(8,128)(2,1)S(1)} fusion(bf16[512,1024]{1,0:T(8,128)(2,1)S(1)} %get-tuple-element.8, bf16[2048,1024]{1,0:T(8,128)(2,1)} %bitcast.20), kind=kOutput, calls=%fused_computation.1 | convolution fusion | flops 2148532224 | bytes 7340032 | tf_op jit(solution)/shard_map/dot_general | solution.py:34
  175.7 1.5 copy.27
  177.2 3.8 %all-to-all-start.6 = ((bf16[4,4,32,2048]{3,2,1,0:T(8,128)(2,1)}), bf16[4,4,32,2048]{3,2,1,0:T(8,128)(2,1)S(1)}, u32[]{:S(2)}, u32[]{:S(2)}) async-start(bf16[4,4,32,2048]{3,2,1,0:T(8,128)(2,1)} %bitcast.67), calls=%async_computation.6 | async-start | bytes 4194304 | tf_op jit(solution)/shard_map/all_to_all | solution.py:21
  181.0 24.7 %all-to-all-done.6 = bf16[4,4,32,2048]{3,2,1,0:T(8,128)(2,1)S(1)} async-done(((bf16[4,4,32,2048]{3,2,1,0:T(8,128)(2,1)}), bf16[4,4,32,2048]{3,2,1,0:T(8,128)(2,1)S(1)}, u32[]{:S(2)}, u32[]{:S(2)}) %all-to-all-start.6) | async-done | bytes 2097184 | tf_op jit(solution)/shard_map/all_to_all | solution.py:21
  206.3 5.4 %collective-permute-start.5 = (bf16[32,2048]{1,0:T(8,128)(2,1)S(1)}, bf16[32,2048]{1,0:T(8,128)(2,1)S(1)}, u32[]{:S(2)}, u32[]{:S(2)}) collective-permute-start(bf16[32,2048]{1,0:T(8,128)(2,1)S(1)} %get-tuple-element.13), channel_id=1, source_target_pairs={{0,12},{4,16},{8,20},{12,24},{16,28},{20,32},{24,36},{28,40},{32,4... | collective-permute-start | bytes 393224 | tf_op jit(solution)/shard_map/ppermute | solution.py:30
  211.7 4.7 %collective-permute-start.4 = (bf16[32,2048]{1,0:T(8,128)(2,1)S(1)}, bf16[32,2048]{1,0:T(8,128)(2,1)S(1)}, u32[]{:S(2)}, u32[]{:S(2)}) collective-permute-start(bf16[32,2048]{1,0:T(8,128)(2,1)S(1)} %get-tuple-element.14), channel_id=1, source_target_pairs={{0,8},{4,12},{8,16},{12,20},{16,24},{20,28},{24,32},{28,36},{32,40... | collective-permute-start | bytes 393224 | tf_op jit(solution)/shard_map/ppermute | solution.py:30
  216.4 2.4 collective-permute-start.3
  218.8 6.7 %collective-permute-done.5 = bf16[32,2048]{1,0:T(8,128)(2,1)S(1)} collective-permute-done((bf16[32,2048]{1,0:T(8,128)(2,1)S(1)}, bf16[32,2048]{1,0:T(8,128)(2,1)S(1)}, u32[]{:S(2)}, u32[]{:S(2)}) %collective-permute-start.5) | collective-permute-done | bytes 131104 | tf_op jit(solution)/shard_map/ppermute | solution.py:30
  225.5 7.5 %collective-permute-done.4 = bf16[32,2048]{1,0:T(8,128)(2,1)S(1)} collective-permute-done((bf16[32,2048]{1,0:T(8,128)(2,1)S(1)}, bf16[32,2048]{1,0:T(8,128)(2,1)S(1)}, u32[]{:S(2)}, u32[]{:S(2)}) %collective-permute-start.4) | collective-permute-done | bytes 131104 | tf_op jit(solution)/shard_map/ppermute | solution.py:30
  233.0 1.9 collective-permute-done.3
  236.5 9.8 %all_to_all.35 = bf16[4,128,512]{2,1,0:T(8,128)(2,1)S(1)} all-to-all(bf16[4,128,512]{2,1,0:T(8,128)(2,1)S(1)} %broadcast_in_dim.18), channel_id=1, replica_groups=mesh['x'=4,'yh'=4,'z'=8,'yl'=2,'core'=2] {'x'}, dimensions={0} | all-to-all | bytes 1048576 | tf_op jit(solution)/shard_map/all_to_all | solution.py:21
  246.7 32.1 %all_to_all.36 = bf16[32,16,512]{2,1,0:T(8,128)(2,1)S(1)} all-to-all(bf16[32,16,512]{2,1,0:T(8,128)(2,1)S(1)} %bitcast.71), channel_id=1, replica_groups=mesh['x'=4,'yh'=4,'z'=8,'yl'=2,'core'=2] {'yh','z'}, dimensions={0} | all-to-all | bytes 1048576 | tf_op jit(solution)/shard_map/all_to_all | solution.py:21
  279.5 3.2 %copy.28 = bf16[2,4,2,32,2048]{4,3,2,1,0:T(8,128)(2,1)} copy(bf16[2,4,2,32,2048]{4,3,1,0,2:T(8,128)(2,1)} %bitcast.72) | data formatting | bytes 4194304 | tf_op jit(solution)/shard_map/transpose | solution.py:138
  (40 shorter events, 11.5 us)
Async XLA Ops:
  7.2 7.5 %copy-start.1 = (bf16[16,512]{1,0:T(8,128)(2,1)S(1)}, bf16[16,512]{1,0:T(8,128)(2,1)}, u32[]{:S(2)}) copy-start(bf16[16,512]{1,0:T(8,128)(2,1)} %param.9) | copy-start | bytes 49156
  7.2 7.5 %copy-start.2 = (bf16[16,512]{1,0:T(8,128)(2,1)S(1)}, bf16[16,512]{1,0:T(8,128)(2,1)}, u32[]{:S(2)}) copy-start(bf16[16,512]{1,0:T(8,128)(2,1)} %param.11) | copy-start | bytes 49156
  7.2 7.5 %copy-start.3 = (bf16[16,512]{1,0:T(8,128)(2,1)S(1)}, bf16[16,512]{1,0:T(8,128)(2,1)}, u32[]{:S(2)}) copy-start(bf16[16,512]{1,0:T(8,128)(2,1)} %param.10) | copy-start | bytes 49156
  9.8 11.8 %all-to-all-start.1 = ((bf16[4,128,512]{1,2,0:T(8,128)(2,1)}), bf16[4,128,512]{1,2,0:T(8,128)(2,1)S(1)}, u32[]{:S(2)}, u32[]{:S(2)}) async-start(bf16[4,128,512]{1,2,0:T(8,128)(2,1)} %bitcast.1), calls=%async_computation.1 | async-start | bytes 1048576 | tf_op jit(solution)/shard_map/all_to_all | solution.py:21
  22.9 59.4 %all-to-all-start = ((bf16[32,16,1536]{2,1,0:T(8,128)(2,1)}), bf16[32,16,1536]{2,1,0:T(8,128)(2,1)S(1)}, u32[]{:S(2)}, u32[]{:S(2)}) async-start(bf16[32,16,1536]{2,1,0:T(8,128)(2,1)} %broadcast_in_dim.16), calls=%async_computation | async-start | bytes 3145728 | tf_op jit(solution)/shard_map/all_to_all | solution.py:21
  82.3 5.7 %copy-start.4 = (s32[1,4]{1,0:T(1,128)S(1)}, s32[1,4]{1,0:T(1,128)}, u32[]{:S(2)}) copy-start(s32[1,4]{1,0:T(1,128)} %param.12) | copy-start | bytes 52
  83.7 18.5 %all-to-all-start.2 = ((f32[4,128,512]{2,1,0:T(8,128)}), f32[4,128,512]{2,1,0:T(8,128)}, u32[]{:S(2)}, u32[]{:S(2)}) async-start(f32[4,128,512]{2,1,0:T(8,128)} %bitcast.4), calls=%async_computation.2 | async-start | bytes 2097152 | tf_op jit(solution)/shard_map/all_to_all | solution.py:21
  104.8 58.7 %all-to-all-start.3 = ((bf16[4,512,1024]{2,1,0:T(8,128)(2,1)}), bf16[4,512,1024]{2,1,0:T(8,128)(2,1)}, u32[]{:S(2)}, u32[]{:S(2)}) async-start(bf16[4,512,1024]{2,1,0:T(8,128)(2,1)} %broadcast_in_dim.17), calls=%async_computation.3 | async-start | bytes 8388608 | tf_op jit(solution)/shard_map/all_to_all | solution.py:21
  109.6 50.8 %all-gather.6.cloned.1.call-start = ((), (), s32[]{:S(2)}) async-start(), calls=%async_computation.8 | async-start | bytes 1966080 | tf_op jit(solution)/shard_map/all_gather | solution.py:113
  110.9 15.0 %collective-permute-start.2 = (bf16[32,2048]{1,0:T(8,128)(2,1)S(1)}, bf16[32,2048]{1,0:T(8,128)(2,1)S(1)}, u32[]{:S(2)}, u32[]{:S(2)}) collective-permute-start(bf16[32,2048]{1,0:T(8,128)(2,1)S(1)} %get-tuple-element.10), channel_id=1, source_target_pairs={{0,500},{4,504},{8,508},{12,0},{16,4},{20,8},{24,12},{28,16},{32,2... | collective-permute-start | bytes 393224 | tf_op jit(solution)/shard_map/ppermute | solution.py:30
  115.1 16.0 %collective-permute-start.1 = (bf16[32,2048]{1,0:T(8,128)(2,1)S(1)}, bf16[32,2048]{1,0:T(8,128)(2,1)S(1)}, u32[]{:S(2)}, u32[]{:S(2)}) collective-permute-start(bf16[32,2048]{1,0:T(8,128)(2,1)S(1)} %get-tuple-element.11), channel_id=1, source_target_pairs={{0,504},{4,508},{8,0},{12,4},{16,8},{20,12},{24,16},{28,20},{32,24... | collective-permute-start | bytes 393224 | tf_op jit(solution)/shard_map/ppermute | solution.py:30
  117.0 17.1 %collective-permute-start = (bf16[32,2048]{1,0:T(8,128)(2,1)S(1)}, bf16[32,2048]{1,0:T(8,128)(2,1)S(1)}, u32[]{:S(2)}, u32[]{:S(2)}) collective-permute-start(bf16[32,2048]{1,0:T(8,128)(2,1)S(1)} %get-tuple-element.9), channel_id=1, source_target_pairs={{0,508},{4,0},{8,4},{12,8},{16,12},{20,16},{24,20},{28,24},{32,28}... | collective-permute-start | bytes 393224 | tf_op jit(solution)/shard_map/ppermute | solution.py:30
  163.5 4.6 %copy-start = (bf16[2,64,512]{2,1,0:T(8,128)(2,1)S(1)}, bf16[2,64,512]{2,1,0:T(8,128)(2,1)}, u32[]{:S(2)}) copy-start(bf16[2,64,512]{2,1,0:T(8,128)(2,1)} %param.13) | copy-start | bytes 393220
  177.2 28.6 %all-to-all-start.6 = ((bf16[4,4,32,2048]{3,2,1,0:T(8,128)(2,1)}), bf16[4,4,32,2048]{3,2,1,0:T(8,128)(2,1)S(1)}, u32[]{:S(2)}, u32[]{:S(2)}) async-start(bf16[4,4,32,2048]{3,2,1,0:T(8,128)(2,1)} %bitcast.67), calls=%async_computation.6 | async-start | bytes 4194304 | tf_op jit(solution)/shard_map/all_to_all | solution.py:21
  180.9 98.6 %all-gather.4.cloned.1.call-start = ((), (), s32[]{:S(2)}) async-start(), calls=%async_computation.7 | async-start | bytes 2621440 | tf_op jit(solution)/shard_map/all_gather | solution.py:137
  206.3 19.2 %collective-permute-start.5 = (bf16[32,2048]{1,0:T(8,128)(2,1)S(1)}, bf16[32,2048]{1,0:T(8,128)(2,1)S(1)}, u32[]{:S(2)}, u32[]{:S(2)}) collective-permute-start(bf16[32,2048]{1,0:T(8,128)(2,1)S(1)} %get-tuple-element.13), channel_id=1, source_target_pairs={{0,12},{4,16},{8,20},{12,24},{16,28},{20,32},{24,36},{28,40},{32,4... | collective-permute-start | bytes 393224 | tf_op jit(solution)/shard_map/ppermute | solution.py:30
  211.7 21.3 %collective-permute-start.4 = (bf16[32,2048]{1,0:T(8,128)(2,1)S(1)}, bf16[32,2048]{1,0:T(8,128)(2,1)S(1)}, u32[]{:S(2)}, u32[]{:S(2)}) collective-permute-start(bf16[32,2048]{1,0:T(8,128)(2,1)S(1)} %get-tuple-element.14), channel_id=1, source_target_pairs={{0,8},{4,12},{8,16},{12,20},{16,24},{20,28},{24,32},{28,36},{32,40... | collective-permute-start | bytes 393224 | tf_op jit(solution)/shard_map/ppermute | solution.py:30
  216.4 18.5 %collective-permute-start.3 = (bf16[32,2048]{1,0:T(8,128)(2,1)S(1)}, bf16[32,2048]{1,0:T(8,128)(2,1)S(1)}, u32[]{:S(2)}, u32[]{:S(2)}) collective-permute-start(bf16[32,2048]{1,0:T(8,128)(2,1)S(1)} %get-tuple-element.15), channel_id=1, source_target_pairs={{0,4},{4,8},{8,12},{12,16},{16,20},{20,24},{24,28},{28,32},{32,36}... | collective-permute-start | bytes 393224 | tf_op jit(solution)/shard_map/ppermute | solution.py:30
Sparse Core Ops, SparseCore 0:
  135.1 25.2 all-gather.5
  236.6 40.9 all-gather.3

commit v2 on v1

v2 whole, which is shorter than its diff:
```python
import jax
import jax.numpy as jnp
from jax import lax
from jax.experimental import pallas as pl
from jax.experimental.pallas import tpu as pltpu
from jax.sharding import Mesh, PartitionSpec as P

HEAD_DIM = 64
SCALE = 0.125
LOW = jnp.bfloat16
WIDE = jnp.float32
AXES = ("x", "yh", "z", "yl", "core")
SIZES = (4, 4, 8, 2, 2)
ENC = ("x", "yh", "z")
PLANE = ("yh", "z")
DEC = ("yl", "core")
GROUP = 256
MIB = 1024 * 1024
VMEM = pl.BlockSpec(memory_space=pltpu.VMEM)
SMEM = pl.BlockSpec(memory_space=pltpu.SMEM)
ANY = pl.BlockSpec(memory_space=pl.ANY)


def exchange(x, axis):
    return lax.all_to_all(x, axis, split_axis=0, concat_axis=0, tiled=True)


def spread(x, axis, size):
    return exchange(jnp.broadcast_to(x[None], (size,) + x.shape), axis)


def shifted(x, axis, by):
    size = 1
    for name in (axis,) if isinstance(axis, str) else axis:
        size *= SIZES[AXES.index(name)]
    return lax.ppermute(x, axis, [(i, (i + by) % size) for i in range(size)])


def dot(a, b, contract):
    return lax.dot_general(a, b, ((contract[:1], contract[1:]), ((), ())), preferred_element_type=WIDE)


def call(kernel, out, ins, specs, out_specs, flops=0, moved=1 << 20, scratch=(), limit=16):
    return pl.pallas_call(
        kernel,
        out_shape=out,
        in_specs=specs,
        out_specs=out_specs,
        scratch_shapes=scratch,
        compiler_params=pltpu.CompilerParams(vmem_limit_bytes=limit * MIB),
        cost_estimate=pl.CostEstimate(flops=flops, bytes_accessed=moved, transcendentals=0),
    )(*ins)


X, YL, CORE = 4, 5, 6


def passages_kernel(scalar, enc_ref, own_ref, near_ref, own_other_ref, near_other_ref, out_ref):
    keys = enc_ref.shape[1]
    length = keys // 4
    half = length // 2
    quarter = out_ref.shape[2]
    yl, core = scalar[YL], scalar[CORE]
    first = pl.multiple_of(scalar[0] * length, length)
    parts = ((own_ref, core, yl), (near_ref, core, 1 - yl), (own_other_ref, 1 - core, yl), (near_other_ref, 1 - core, 1 - yl))
    for k in range(4):
        columns = pl.ds(pl.multiple_of(lax.rem(scalar[X] + k, 4) * quarter, quarter), quarter)
        for b in range(2):
            out_ref[k, pl.ds(b * keys, length), :] = enc_ref[b, pl.ds(first, length), columns]
        for part, b, place in parts:
            for j in range(1, 4):
                rows = pl.multiple_of(b * keys + j * length + place * half, half)
                out_ref[k, pl.ds(rows, half), :] = part[j - 1, :, columns]


def attention_kernel(q_ref, kv_ref, grad_ref, ctx_ref, gq_ref, gkv_ref):
    rows, width = q_ref.shape
    batches = 2
    queries = rows // batches
    keys = kv_ref.shape[0] // batches
    heads = GROUP // HEAD_DIM
    row_head = lax.broadcasted_iota(jnp.int32, (heads * queries, GROUP), 0) // queries
    col_head = lax.broadcasted_iota(jnp.int32, (heads * queries, GROUP), 1) // HEAD_DIM
    own = row_head == col_head
    col_small = lax.broadcasted_iota(jnp.int32, (queries, GROUP), 1) // HEAD_DIM

    def per_head(x):
        return jnp.where(own, jnp.concatenate([x] * heads, axis=0), jnp.zeros((), x.dtype))

    def merged(x):
        out = x[:queries]
        for h in range(1, heads):
            out = jnp.where(col_small == h, x[h * queries : (h + 1) * queries], out)
        return out

    for b in range(batches):
        for g in range(width // GROUP):
            qs, ks = pl.ds(b * queries, queries), pl.ds(b * keys, keys)
            cs, vs = pl.ds(g * GROUP, GROUP), pl.ds(width + g * GROUP, GROUP)
            query = per_head(q_ref[qs, cs])
            grad = per_head(grad_ref[qs, cs])
            key, value = kv_ref[ks, cs], kv_ref[ks, vs]
            scores = dot(query, key, (1, 1)) * SCALE
            raw = jnp.exp(scores - jnp.max(scores, axis=-1, keepdims=True))
            attention = raw / jnp.sum(raw, axis=-1, keepdims=True)
            low = attention.astype(LOW)
            ctx_ref[qs, cs] = merged(dot(low, value, (1, 0))).astype(LOW)
            grad_attention = dot(grad, value, (1, 1))
            correction = jnp.sum(attention * grad_attention, axis=-1, keepdims=True)
            grad_scores = (attention * (grad_attention - correction) * SCALE).astype(LOW)
            gkv_ref[ks, vs] = dot(low, grad, (0, 0)).astype(LOW)
            gkv_ref[ks, cs] = dot(grad_scores, query, (0, 0)).astype(LOW)
            gq_ref[qs, cs] = merged(dot(grad_scores, key, (1, 0))).astype(LOW)


def partial_kernel(other, scalar, grad_ref, *refs):
    out_ref = refs[-1]
    rows = out_ref.shape[0]
    batch = 1 - scalar[CORE] if other else scalar[CORE]
    grad = grad_ref[pl.ds(pl.multiple_of(batch * rows, rows), rows), :]
    quarter = out_ref.shape[1] // 4
    for (k, offset), weight in zip(PIECES, refs):
        start = pl.multiple_of(lax.rem(scalar[X] + k, 4) * quarter + offset, 256)
        out_ref[:, pl.ds(start, weight.shape[0])] = dot(grad, weight[...], (1, 1)).astype(LOW)


def place_kernel(scalar, *refs):
    parts, out_ref, sems = refs[:4], refs[4], refs[5]
    half = parts[0].shape[1]
    copies = []
    for i, part in enumerate(parts):
        b = scalar[CORE] if i < 2 else 1 - scalar[CORE]
        place = scalar[YL] if i % 2 == 0 else 1 - scalar[YL]
        for j in range(4):
            rows = pl.multiple_of(scalar[j] * 2 * half + place * half, half)
            copy = pltpu.make_async_copy(part.at[j], out_ref.at[b, pl.ds(rows, half)], sems.at[len(copies)])
            copy.start()
            copies.append(copy)
    for copy in copies:
        copy.wait()


PIECES = ((0, 0), (1, 0), (3, 0), (2, 0), (2, 256))


def around(own):
    above = shifted(own, "x", -1)
    below = shifted(own, "x", 1)
    size = own.shape[0] // 2
    return [own, above, below, shifted(above[:size], "x", -1), shifted(below[size:], "x", 1)]


def project(quarters, pieces):
    total = None
    for (k, offset), piece in zip(PIECES, pieces):
        term = dot(quarters[k][:, offset : offset + piece.shape[0]], piece, (1, 0))
        total = term if total is None else total + term
    return total.astype(LOW)


def on_device(dec_states, enc_states, w_query, w_key, w_value, passage_slot, ctx_grad):
    batches, dec_rows, model = dec_states.shape
    enc_rows = enc_states.shape[1]
    width = w_query.shape[1]
    passages = passage_slot.shape[1]
    length = enc_rows // passages
    half = length // 2
    quarter = model // 4
    rows = batches * dec_rows
    dec_flat = dec_states.reshape(rows, model)
    x, yl, core = lax.axis_index("x"), lax.axis_index("yl"), lax.axis_index("core")
    order = passage_slot[0]
    scalar = jnp.concatenate([order, jnp.stack([x, yl, core, x]).astype(jnp.int32)])
    low = lambda *shape: jax.ShapeDtypeStruct(shape, LOW)

    by_slot = enc_states.reshape(batches, passages, length, model)
    fetched = []
    for j in range(1, passages):
        piece = lax.dynamic_slice(by_slot, (core, order[j], yl * half, 0), (1, 1, half, model))
        fetched.append(shifted(piece.reshape(half, model), ENC, -j))
    dec_parts = []
    for k in range(4):
        part = lax.dynamic_slice_in_dim(dec_flat, ((x + k) % 4) * quarter, quarter, 1)
        dec_parts.append(shifted(part, "x", k) if k else part)
    weights = spread(jnp.concatenate([w_key, w_value, w_query], axis=1), PLANE, 32).reshape(quarter, 3 * width)
    fetched, dec_parts, weights = lax.optimization_barrier((fetched, dec_parts, weights))
    pieces = around(weights[:, : 2 * width])
    dec_quarter = jnp.take(jnp.stack(dec_parts), (x - jnp.arange(4)) % 4, axis=0).reshape(4 * rows, quarter)
    queries = dot(dec_quarter, weights[:, 2 * width :], (1, 0)).reshape(4, rows, width)
    queries = jnp.sum(exchange(queries, "x"), axis=0).astype(LOW)
    own = jnp.stack(fetched)
    near = shifted(own, "yl", 1)
    quarters = call(
        passages_kernel,
        low(4, batches * enc_rows, quarter),
        (scalar, enc_states, own, near, shifted(own, "core", 1), shifted(near, "core", 1)),
        [SMEM] + [VMEM] * 5,
        VMEM,
        moved=4 * MIB,
    )
    kv = project(quarters, pieces)

    context, gq, gkv = call(
        attention_kernel,
        (low(rows, width), low(rows, width), low(*kv.shape)),
        (queries, kv, ctx_grad.reshape(rows, width)),
        [VMEM] * 3,
        (VMEM,) * 3,
        flops=940_000_000,
        moved=3 * MIB,
    )

    def partial(other):
        def kernel(*refs):
            partial_kernel(other, *refs)

        return call(
            kernel,
            low(enc_rows, model),
            (scalar, gkv, *pieces),
            [SMEM] + [VMEM] * 6,
            VMEM,
            flops=1_080_000_000,
            moved=6 * MIB,
        )

    got = shifted(partial(True), "core", 1)
    total = (partial(False).astype(WIDE) + got.astype(WIDE)).astype(LOW).reshape(passages, 2, half, model)
    gq_parts = spread(gq, "x", 4).reshape(4 * rows, width)
    total, gq_parts = lax.optimization_barrier((total, gq_parts))
    got = shifted(lax.dynamic_index_in_dim(total, 1 - yl, 1, False), "yl", 1)
    total = lax.dynamic_index_in_dim(total, yl, 1, False).astype(WIDE) + got.astype(WIDE)
    total = total.astype(LOW)
    back = jnp.stack([shifted(total[j], ENC, j) if j else total[j] for j in range(passages)])
    near = shifted(back, "yl", 1)
    grad_enc = call(
        place_kernel,
        low(batches, enc_rows, model),
        (scalar, back, near, shifted(back, "core", 1), shifted(near, "core", 1)),
        [SMEM] + [ANY] * 4,
        ANY,
        moved=4 * MIB,
        scratch=[pltpu.SemaphoreType.DMA((16,))],
    )

    share = dot(dec_quarter, gq_parts, (0, 0)).astype(LOW).reshape(32, quarter // 32, width)
    grad_query = jnp.sum(exchange(share, PLANE).astype(WIDE), axis=0)
    return context.reshape(batches, dec_rows, width), grad_query, grad_enc


def solution(mesh):
    fine = Mesh(mesh.devices.reshape(SIZES), AXES)
    in_specs = (
        P(None, ENC, None),
        P(None, ENC, None),
        P(ENC, DEC),
        P(ENC, DEC),
        P(ENC, DEC),
        P(ENC, None),
        P(None, ENC, DEC),
    )
    out_specs = (P(None, ENC, DEC), P(ENC, DEC), P(None, ENC, None))
    return jax.shard_map(on_device, mesh=fine, in_specs=in_specs, out_specs=out_specs, check_vma=False)
```

time: 291 us -> 237 us (0.81)
  waiting for transfers between devices: 128 us -> 73 us
  starting transfers between devices: 62.2 us -> 115 us
  blocking collectives: 41.9 us -> 0 us
  between operations: 22 us -> 7.19 us
  Pallas kernels: 3.1 us -> 11.1 us
  matrix products: 11 us -> 8.07 us
    all_to_all x5 -> x4, waiting for transfers between devices: 81.5 us -> 8.56 us  [exchange(): return lax.all_to_all(x, axis, split_axis=0, concat_axis=0, tiled=True)]
    ppermute x6 -> x21, starting transfers between devices: 27.4 us -> 79.3 us  [shifted(): return lax.ppermute(x, axis, [(i, (i + by) % size) for i in range(size)])]
    all_to_all x2 -> x0, blocking collectives: 41.9 us -> none  [exchange(): return lax.all_to_all(x, axis, split_axis=0, concat_axis=0, tiled=True)]
    ppermute x6 -> x21, waiting for transfers between devices: 24.3 us -> 64.4 us  [shifted(): return lax.ppermute(x, axis, [(i, (i + by) % size) for i in range(size)])]
    all_gather x2 -> x0, waiting for transfers between devices: 22.4 us -> none  [the longest x1 22.4 us: on_device(): parts = lax.all_gather(parts, DEC, axis=0, tiled=False)]
    pallas_call x1 -> x5, Pallas kernels: 3.1 us -> 11.1 us  [call(): pl.pallas_call(kernel, out_shape=out, in_specs=specs, out_specs=out_specs...]
    unnamed x10 -> x46, local copies, waits for them, and re-layouts: 0.02 us -> 6.9 us
    transpose x2 -> x0, local copies, waits for them, and re-layouts: 4.67 us -> none  [the longest x1 3.16 us: on_device(): jnp.transpose(back, (1, 2, 0, 3, 4)).reshape(batches, enc_rows, model)]
  transfers between devices with their start and end apart: 13 -> 25, of which waited for: 10 -> 11; matrix products, arithmetic and copies ran while one was open for 3% -> 8% of each run, Pallas kernels for 0% -> 1%
where the time goes in v2:
time: 237 us; the launch traced here: 236 us
  starting transfers between devices  115 us (49%)
  waiting for transfers between devices  73 us (31%)
  local copies, waits for them, and re-layouts  13.7 us (6%)
  Pallas kernels  11.1 us (5%)
  matrix products  8.07 us (3%)
  other arithmetic  7.43 us (3%)
  between operations  7.19 us (3%)
    ppermute x21, starting transfers between devices, shifted(): return lax.ppermute(x, axis, [(i, (i + by) % size) for i in range(size)])  79.3 us
    ppermute x21, waiting for transfers between devices, shifted(): return lax.ppermute(x, axis, [(i, (i + by) % size) for i in range(size)])  64.4 us
    all_to_all x4, starting transfers between devices, exchange(): return lax.all_to_all(x, axis, split_axis=0, concat_axis=0, tiled=True)  35.8 us
    pallas_call x5, Pallas kernels, call(): pl.pallas_call(kernel, out_shape=out, in_specs=specs, out_specs=out_specs...  11.1 us
    all_to_all x4, waiting for transfers between devices, exchange(): return lax.all_to_all(x, axis, split_axis=0, concat_axis=0, tiled=True)  8.56 us
    dot_general x7, matrix products, dot(): lax.dot_general(a, b, ((contract[:1], contract[1:]), ((), ())), preferred...  8.07 us
    unnamed x46, local copies, waits for them, and re-layouts  6.9 us
  transfers between devices with their start and end apart: 25, of which 11 were waited for; matrix products, arithmetic and copies ran while one was open for 8% of the time, Pallas kernels for 1%

profile of v2, /device:TPU:1, one launch (start us, length us, event | category | flops | bytes accessed | tf_op | source)
XLA Modules:
  0.0 235.6 jit_solution(2001345678321209341)
XLA Ops:
  2.7 16.6 %all-to-all-start = ((bf16[32,16,1536]{2,1,0:T(8,128)(2,1)}), bf16[32,16,1536]{2,1,0:T(8,128)(2,1)S(1)}, u32[]{:S(2)}, u32[]{:S(2)}) async-start(bf16[32,16,1536]{2,1,0:T(8,128)(2,1)} %broadcast_in_dim.31), calls=%async_computation | async-start | bytes 3145728 | tf_op jit(solution)/shard_map/all_to_all | solution.py:25
  19.5 3.1 %collective-permute-start.3 = (bf16[128,512]{1,0:T(8,128)(2,1)S(1)}, bf16[128,512]{1,0:T(8,128)(2,1)S(1)}, u32[]{:S(2)}, u32[]{:S(2)}) collective-permute-start(bf16[128,512]{1,0:T(8,128)(2,1)S(1)} %get-tuple-element.38), channel_id=1, source_target_pairs={{0,128},{128,256},{256,384},{384,0},{1,129},{129,257},{257,385},{3... | collective-permute-start | bytes 393224 | tf_op jit(solution)/shard_map/ppermute | solution.py:36
  22.6 4.4 %collective-permute-start.4 = (bf16[128,512]{1,0:T(8,128)(2,1)S(1)}, bf16[128,512]{1,0:T(8,128)(2,1)S(1)}, u32[]{:S(2)}, u32[]{:S(2)}) collective-permute-start(bf16[128,512]{1,0:T(8,128)(2,1)S(1)} %get-tuple-element.37), channel_id=1, source_target_pairs={{0,256},{128,384},{256,0},{384,128},{1,257},{129,385},{257,1},{385... | collective-permute-start | bytes 393224 | tf_op jit(solution)/shard_map/ppermute | solution.py:36
  27.0 3.1 %collective-permute-start.5 = (bf16[128,512]{1,0:T(8,128)(2,1)S(1)}, bf16[128,512]{1,0:T(8,128)(2,1)S(1)}, u32[]{:S(2)}, u32[]{:S(2)}) collective-permute-start(bf16[128,512]{1,0:T(8,128)(2,1)S(1)} %get-tuple-element.36), channel_id=1, source_target_pairs={{0,384},{128,0},{256,128},{384,256},{1,385},{129,1},{257,129},{385... | collective-permute-start | bytes 393224 | tf_op jit(solution)/shard_map/ppermute | solution.py:36
  37.7 7.2 %collective-permute-start = (bf16[32,2048]{1,0:T(8,128)(2,1)S(1)}, bf16[32,2048]{1,0:T(8,128)(2,1)S(1)}, u32[]{:S(2)}, u32[]{:S(2)}) collective-permute-start(bf16[32,2048]{1,0:T(8,128)(2,1)S(1)} %get-tuple-element.31), channel_id=1, source_target_pairs={{0,508},{4,0},{8,4},{12,8},{16,12},{20,16},{24,20},{28,24},{32,28}... | collective-permute-start | bytes 393224 | tf_op jit(solution)/shard_map/ppermute | solution.py:36
  44.9 4.0 %collective-permute-start.1 = (bf16[32,2048]{1,0:T(8,128)(2,1)S(1)}, bf16[32,2048]{1,0:T(8,128)(2,1)S(1)}, u32[]{:S(2)}, u32[]{:S(2)}) collective-permute-start(bf16[32,2048]{1,0:T(8,128)(2,1)S(1)} %get-tuple-element.30), channel_id=1, source_target_pairs={{0,504},{4,508},{8,0},{12,4},{16,8},{20,12},{24,16},{28,20},{32,24... | collective-permute-start | bytes 393224 | tf_op jit(solution)/shard_map/ppermute | solution.py:36
  49.5 3.1 %collective-permute-start.2 = (bf16[32,2048]{1,0:T(8,128)(2,1)S(1)}, bf16[32,2048]{1,0:T(8,128)(2,1)S(1)}, u32[]{:S(2)}, u32[]{:S(2)}) collective-permute-start(bf16[32,2048]{1,0:T(8,128)(2,1)S(1)} %get-tuple-element.29), channel_id=1, source_target_pairs={{0,500},{4,504},{8,508},{12,0},{16,4},{20,8},{24,12},{28,16},{32,2... | collective-permute-start | bytes 393224 | tf_op jit(solution)/shard_map/ppermute | solution.py:36
  52.7 3.3 %collective-permute-done = bf16[32,2048]{1,0:T(8,128)(2,1)S(1)} collective-permute-done((bf16[32,2048]{1,0:T(8,128)(2,1)S(1)}, bf16[32,2048]{1,0:T(8,128)(2,1)S(1)}, u32[]{:S(2)}, u32[]{:S(2)}) %collective-permute-start) | collective-permute-done | bytes 131104 | tf_op jit(solution)/shard_map/ppermute | solution.py:36
  56.0 21.8 %collective-permute-done.1 = bf16[32,2048]{1,0:T(8,128)(2,1)S(1)} collective-permute-done((bf16[32,2048]{1,0:T(8,128)(2,1)S(1)}, bf16[32,2048]{1,0:T(8,128)(2,1)S(1)}, u32[]{:S(2)}, u32[]{:S(2)}) %collective-permute-start.1) | collective-permute-done | bytes 131104 | tf_op jit(solution)/shard_map/ppermute | solution.py:36
  79.2 4.8 %collective-permute-start.10 = (bf16[512,1024]{1,0:T(8,128)(2,1)S(1)}, bf16[512,1024]{1,0:T(8,128)(2,1)S(1)}, u32[]{:S(2)}, u32[]{:S(2)}) collective-permute-start(bf16[512,1024]{1,0:T(8,128)(2,1)S(1)} %slice.60.refs_2_), channel_id=1, source_target_pairs={{0,128},{128,256},{256,384},{384,0},{1,129},{129,257},{257,385},{3... | collective-permute-start | bytes 3145736 | tf_op jit(solution)/shard_map/ppermute | solution.py:36
  84.0 4.0 %collective-permute-start.9 = (bf16[512,1024]{1,0:T(8,128)(2,1)S(1)}, bf16[512,1024]{1,0:T(8,128)(2,1)S(1)}, u32[]{:S(2)}, u32[]{:S(2)}) collective-permute-start(bf16[512,1024]{1,0:T(8,128)(2,1)S(1)} %slice.60.refs_2_), channel_id=1, source_target_pairs={{0,384},{128,0},{256,128},{384,256},{1,385},{129,1},{257,129},{385... | collective-permute-start | bytes 3145736 | tf_op jit(solution)/shard_map/ppermute | solution.py:36
  88.9 2.4 %gather_fusion = bf16[4,128,512]{2,1,0:T(8,128)(2,1)} fusion(bf16[4,128,512]{2,1,0:T(8,128)(2,1)} %pad_maximum_fusion, s32[1024]{0:T(1024)S(1)} %pad_clamp_fusion), kind=kCustom, calls=%fused_computation | custom fusion | bytes 1048592 | tf_op jit(solution)/shard_map/jit(_take)/gather | solution.py:188
  91.3 2.7 %fusion.3 = f32[4,128,512]{2,1,0:T(8,128)} fusion(bf16[512,1536]{1,0:T(8,128)(2,1)} %bitcast.71, bf16[4,128,512]{2,1,0:T(8,128)(2,1)} %gather_fusion, pred[4]{0:T(512)(128)(4,1)S(1)} %compare_and_fusion), kind=kOutput, calls=%fused_computation.16 | convolution fusion | flops 268697600 | bytes 2097156 | tf_op jit(solution)/shard_map/dot_general | solution.py:40
  93.9 4.2 %all-to-all-start.1 = ((f32[4,128,512]{2,1,0:T(8,128)}), f32[4,128,512]{2,1,0:T(8,128)}, u32[]{:S(2)}, u32[]{:S(2)}) async-start(f32[4,128,512]{2,1,0:T(8,128)} %fusion.3), calls=%async_computation.1 | async-start | bytes 2097152 | tf_op jit(solution)/shard_map/all_to_all | solution.py:25
  101.2 3.4 %collective-permute-start.7 = (bf16[3,32,2048]{2,1,0:T(8,128)(2,1)S(1)}, bf16[3,32,2048]{2,1,0:T(8,128)(2,1)}, u32[]{:S(2)}, u32[]{:S(2)}) collective-permute-start(bf16[3,32,2048]{2,1,0:T(8,128)(2,1)S(1)} %pad_maximum_fusion.2.own_ref), channel_id=1, source_target_pairs={{0,1},{1,0},{2,3},{3,2},{4,5},{5,4},{6,7},{7,6},{8,9},{9,8},{10,11... | collective-permute-start | bytes 1179656 | tf_op jit(solution)/shard_map/ppermute | solution.py:36
  104.6 5.8 %collective-permute-done.6.near_ref = bf16[3,32,2048]{2,1,0:T(8,128)(2,1)} collective-permute-done((bf16[3,32,2048]{2,1,0:T(8,128)(2,1)S(1)}, bf16[3,32,2048]{2,1,0:T(8,128)(2,1)}, u32[]{:S(2)}, u32[]{:S(2)}) %collective-permute-start.6) | collective-permute-done | bytes 393248 | tf_op jit(solution)/shard_map/ppermute | solution.py:36
  110.4 4.3 %collective-permute-start.8 = (bf16[3,32,2048]{2,1,0:T(8,128)(2,1)}, bf16[3,32,2048]{2,1,0:T(8,128)(2,1)}, u32[]{:S(2)}, u32[]{:S(2)}) collective-permute-start(bf16[3,32,2048]{2,1,0:T(8,128)(2,1)} %collective-permute-done.6.near_ref), channel_id=1, source_target_pairs={{0,1},{1,0},{2,3},{3,2},{4,5},{5,4},{6,7},{7,6},{8,9},{9,8},{10,11... | collective-permute-start | bytes 1179656 | tf_op jit(solution)/shard_map/ppermute | solution.py:36
  114.8 5.7 %all-to-all-done.1 = f32[4,128,512]{2,1,0:T(8,128)} async-done(((f32[4,128,512]{2,1,0:T(8,128)}), f32[4,128,512]{2,1,0:T(8,128)}, u32[]{:S(2)}, u32[]{:S(2)}) %all-to-all-start.1) | async-done | bytes 1048608 | tf_op jit(solution)/shard_map/all_to_all | solution.py:25
  125.6 5.1 %collective-permute-start.11 = (bf16[256,1024]{1,0:T(8,128)(2,1)S(1)}, bf16[256,1024]{1,0:T(8,128)(2,1)S(1)}, u32[]{:S(2)}, u32[]{:S(2)}) collective-permute-start(bf16[256,1024]{1,0:T(8,128)(2,1)S(1)} %slice.79), channel_id=1, source_target_pairs={{0,384},{128,0},{256,128},{384,256},{1,385},{129,1},{257,129},{385... | collective-permute-start | bytes 1572872 | tf_op jit(solution)/shard_map/ppermute | solution.py:36
  134.1 5.7 %collective-permute-done.11.refs_5_ = bf16[256,1024]{1,0:T(8,128)(2,1)S(1)} collective-permute-done((bf16[256,1024]{1,0:T(8,128)(2,1)S(1)}, bf16[256,1024]{1,0:T(8,128)(2,1)S(1)}, u32[]{:S(2)}, u32[]{:S(2)}) %collective-permute-start.11) | collective-permute-done | bytes 524320 | tf_op jit(solution)/shard_map/ppermute | solution.py:36
  140.3 4.3 %collective-permute-done.12.refs_6_ = bf16[256,1024]{1,0:T(8,128)(2,1)S(1)} collective-permute-done((bf16[256,1024]{1,0:T(8,128)(2,1)S(1)}, bf16[256,1024]{1,0:T(8,128)(2,1)S(1)}, u32[]{:S(2)}, u32[]{:S(2)}) %collective-permute-start.12) | collective-permute-done | bytes 524320 | tf_op jit(solution)/shard_map/ppermute | solution.py:36
  146.0 3.1 %shard_map.95 = (bf16[128,512]{1,0:T(8,128)(2,1)}, bf16[128,512]{1,0:T(8,128)(2,1)S(1)}, bf16[512,1024]{1,0:T(8,128)(2,1)S(1)}) custom-call(bf16[128,512]{1,0:T(8,128)(2,1)S(1)} %copy-done.7, bf16[512,1024]{1,0:T(8,128)(2,1)S(1)} %add_convert_fusion.1.kv_ref, bf16[128,512]{1,0:T(8,128)(2,1)S(1)} %bitcast.69), custom_call_target="tpu_custom_call" | custom-call | flops 940000000 | bytes 3145728 | tf_op jit(solution)/shard_map/pallas_call | solution.py:44
  149.1 2.8 %shard_map.97 = bf16[256,2048]{1,0:T(8,128)(2,1)} custom-call(s32[8]{0:T(128)S(1)} %concatenate.7.scalar.refs_0_, bf16[512,1024]{1,0:T(8,128)(2,1)S(1)} %get-tuple-element.25.refs_1_, bf16[512,1024]{1,0:T(8,128)(2,1)S(1)} %slice.60.refs_2_, bf16[512,1024]{1,0:T(8,128)(2,1)S(1)} %collective-permute-done.9.refs_3_, ...), custom_call_target="tpu_custom_call" | custom-call | flops 1080000000 | bytes 6291456 | tf_op jit(solution)/shard_map/pallas_call | solution.py:44
  151.9 5.5 %collective-permute-start.13 = (bf16[256,2048]{1,0:T(8,128)(2,1)}, bf16[256,2048]{1,0:T(8,128)(2,1)}, u32[]{:S(2)}, u32[]{:S(2)}) collective-permute-start(bf16[256,2048]{1,0:T(8,128)(2,1)} %shard_map.97), channel_id=1, source_target_pairs={{0,1},{1,0},{2,3},{3,2},{4,5},{5,4},{6,7},{7,6},{8,9},{9,8},{10,11... | collective-permute-start | bytes 3145736 | tf_op jit(solution)/shard_map/ppermute | solution.py:36
  158.3 4.1 %all-to-all-start.2 = ((bf16[4,128,512]{2,1,0:T(8,128)(2,1)}), bf16[4,128,512]{2,1,0:T(8,128)(2,1)}, u32[]{:S(2)}, u32[]{:S(2)}) async-start(bf16[4,128,512]{2,1,0:T(8,128)(2,1)} %broadcast_in_dim.37), calls=%async_computation.2 | async-start | bytes 1048576 | tf_op jit(solution)/shard_map/all_to_all | solution.py:25
  169.3 2.9 %all-to-all-done.2 = bf16[4,128,512]{2,1,0:T(8,128)(2,1)} async-done(((bf16[4,128,512]{2,1,0:T(8,128)(2,1)}), bf16[4,128,512]{2,1,0:T(8,128)(2,1)}, u32[]{:S(2)}, u32[]{:S(2)}) %all-to-all-start.2) | async-done | bytes 524320 | tf_op jit(solution)/shard_map/all_to_all | solution.py:25
  174.3 12.4 %collective-permute-done.14 = bf16[4,32,2048]{2,1,0:T(8,128)(2,1)S(1)} collective-permute-done((bf16[4,32,2048]{2,1,0:T(8,128)(2,1)S(1)}, bf16[4,32,2048]{2,1,0:T(8,128)(2,1)S(1)}, u32[]{:S(2)}, u32[]{:S(2)}) %collective-permute-start.14) | collective-permute-done | bytes 524320 | tf_op jit(solution)/shard_map/ppermute | solution.py:36
  195.0 10.8 %all-to-all-start.3 = ((bf16[32,16,512]{2,1,0:T(8,128)(2,1)}), bf16[32,16,512]{2,1,0:T(8,128)(2,1)S(1)}, u32[]{:S(2)}, u32[]{:S(2)}) async-start(bf16[32,16,512]{2,1,0:T(8,128)(2,1)} %bitcast.32), calls=%async_computation.3 | async-start | bytes 1048576 | tf_op jit(solution)/shard_map/all_to_all | solution.py:25
  205.8 3.5 %collective-permute-done.17 = bf16[32,2048]{1,0:T(8,128)(2,1)S(1)} collective-permute-done((bf16[32,2048]{1,0:T(8,128)(2,1)S(1)}, bf16[32,2048]{1,0:T(8,128)(2,1)S(1)}, u32[]{:S(2)}, u32[]{:S(2)}) %collective-permute-start.17) | collective-permute-done | bytes 131104 | tf_op jit(solution)/shard_map/ppermute | solution.py:36
  211.5 8.5 %collective-permute-start.19 = (bf16[4,32,2048]{2,1,0:T(8,128)(2,1)S(1)}, bf16[4,32,2048]{2,1,0:T(8,128)(2,1)S(1)}, u32[]{:S(2)}, u32[]{:S(2)}) collective-permute-start(bf16[4,32,2048]{2,1,0:T(8,128)(2,1)S(1)} %pad_maximum_fusion.1.refs_0_), channel_id=1, source_target_pairs={{0,1},{1,0},{2,3},{3,2},{4,5},{5,4},{6,7},{7,6},{8,9},{9,8},{10,11... | collective-permute-start | bytes 1572872 | tf_op jit(solution)/shard_map/ppermute | solution.py:36
  220.0 6.8 %collective-permute-done.18.refs_1_ = bf16[4,32,2048]{2,1,0:T(8,128)(2,1)S(1)} collective-permute-done((bf16[4,32,2048]{2,1,0:T(8,128)(2,1)S(1)}, bf16[4,32,2048]{2,1,0:T(8,128)(2,1)S(1)}, u32[]{:S(2)}, u32[]{:S(2)}) %collective-permute-start.18) | collective-permute-done | bytes 524320 | tf_op jit(solution)/shard_map/ppermute | solution.py:36
  226.8 5.3 %collective-permute-start.20 = (bf16[4,32,2048]{2,1,0:T(8,128)(2,1)S(1)}, bf16[4,32,2048]{2,1,0:T(8,128)(2,1)S(1)}, u32[]{:S(2)}, u32[]{:S(2)}) collective-permute-start(bf16[4,32,2048]{2,1,0:T(8,128)(2,1)S(1)} %collective-permute-done.18.refs_1_), channel_id=1, source_target_pairs={{0,1},{1,0},{2,3},{3,2},{4,5},{5,4},{6,7},{7,6},{8,9},{9,8},{10,11... | collective-permute-start | bytes 1572872 | tf_op jit(solution)/shard_map/ppermute | solution.py:36
  (102 shorter events, 43.9 us)
Async XLA Ops:
  1.4 18.0 %copy-start.12 = (bf16[2,64,2048]{2,1,0:T(8,128)(2,1)S(1)}, bf16[2,64,2048]{2,1,0:T(8,128)(2,1)}, u32[]{:S(2)}) copy-start(bf16[2,64,2048]{2,1,0:T(8,128)(2,1)} %param.7) | copy-start | bytes 1572868
  2.7 27.3 %copy-start.22 = (s32[1,4]{1,0:T(1,128)S(1)}, s32[1,4]{1,0:T(1,128)}, u32[]{:S(2)}) copy-start(s32[1,4]{1,0:T(1,128)} %param.12) | copy-start | bytes 52
  2.7 75.1 %all-to-all-start = ((bf16[32,16,1536]{2,1,0:T(8,128)(2,1)}), bf16[32,16,1536]{2,1,0:T(8,128)(2,1)S(1)}, u32[]{:S(2)}, u32[]{:S(2)}) async-start(bf16[32,16,1536]{2,1,0:T(8,128)(2,1)} %broadcast_in_dim.31), calls=%async_computation | async-start | bytes 3145728 | tf_op jit(solution)/shard_map/all_to_all | solution.py:25
  19.5 29.4 %collective-permute-start.3 = (bf16[128,512]{1,0:T(8,128)(2,1)S(1)}, bf16[128,512]{1,0:T(8,128)(2,1)S(1)}, u32[]{:S(2)}, u32[]{:S(2)}) collective-permute-start(bf16[128,512]{1,0:T(8,128)(2,1)S(1)} %get-tuple-element.38), channel_id=1, source_target_pairs={{0,128},{128,256},{256,384},{384,0},{1,129},{129,257},{257,385},{3... | collective-permute-start | bytes 393224 | tf_op jit(solution)/shard_map/ppermute | solution.py:36
  22.6 30.0 %collective-permute-start.4 = (bf16[128,512]{1,0:T(8,128)(2,1)S(1)}, bf16[128,512]{1,0:T(8,128)(2,1)S(1)}, u32[]{:S(2)}, u32[]{:S(2)}) collective-permute-start(bf16[128,512]{1,0:T(8,128)(2,1)S(1)} %get-tuple-element.37), channel_id=1, source_target_pairs={{0,256},{128,384},{256,0},{384,128},{1,257},{129,385},{257,1},{385... | collective-permute-start | bytes 393224 | tf_op jit(solution)/shard_map/ppermute | solution.py:36
  27.0 25.7 %collective-permute-start.5 = (bf16[128,512]{1,0:T(8,128)(2,1)S(1)}, bf16[128,512]{1,0:T(8,128)(2,1)S(1)}, u32[]{:S(2)}, u32[]{:S(2)}) collective-permute-start(bf16[128,512]{1,0:T(8,128)(2,1)S(1)} %get-tuple-element.36), channel_id=1, source_target_pairs={{0,384},{128,0},{256,128},{384,256},{1,385},{129,1},{257,129},{385... | collective-permute-start | bytes 393224 | tf_op jit(solution)/shard_map/ppermute | solution.py:36
  37.7 18.3 %collective-permute-start = (bf16[32,2048]{1,0:T(8,128)(2,1)S(1)}, bf16[32,2048]{1,0:T(8,128)(2,1)S(1)}, u32[]{:S(2)}, u32[]{:S(2)}) collective-permute-start(bf16[32,2048]{1,0:T(8,128)(2,1)S(1)} %get-tuple-element.31), channel_id=1, source_target_pairs={{0,508},{4,0},{8,4},{12,8},{16,12},{20,16},{24,20},{28,24},{32,28}... | collective-permute-start | bytes 393224 | tf_op jit(solution)/shard_map/ppermute | solution.py:36
  44.9 33.0 %collective-permute-start.1 = (bf16[32,2048]{1,0:T(8,128)(2,1)S(1)}, bf16[32,2048]{1,0:T(8,128)(2,1)S(1)}, u32[]{:S(2)}, u32[]{:S(2)}) collective-permute-start(bf16[32,2048]{1,0:T(8,128)(2,1)S(1)} %get-tuple-element.30), channel_id=1, source_target_pairs={{0,504},{4,508},{8,0},{12,4},{16,8},{20,12},{24,16},{28,20},{32,24... | collective-permute-start | bytes 393224 | tf_op jit(solution)/shard_map/ppermute | solution.py:36
  49.5 28.3 %collective-permute-start.2 = (bf16[32,2048]{1,0:T(8,128)(2,1)S(1)}, bf16[32,2048]{1,0:T(8,128)(2,1)S(1)}, u32[]{:S(2)}, u32[]{:S(2)}) collective-permute-start(bf16[32,2048]{1,0:T(8,128)(2,1)S(1)} %get-tuple-element.29), channel_id=1, source_target_pairs={{0,500},{4,504},{8,508},{12,0},{16,4},{20,8},{24,12},{28,16},{32,2... | collective-permute-start | bytes 393224 | tf_op jit(solution)/shard_map/ppermute | solution.py:36
  52.6 25.2 %copy-start.18 = (bf16[128,512]{1,0:T(8,128)(2,1)}, bf16[128,512]{1,0:T(8,128)(2,1)S(1)}, u32[]{:S(2)}) copy-start(bf16[128,512]{1,0:T(8,128)(2,1)S(1)} %collective-permute-done.4) | copy-start | bytes 393220
  52.7 25.2 %copy-start.20 = (bf16[128,512]{1,0:T(8,128)(2,1)}, bf16[128,512]{1,0:T(8,128)(2,1)S(1)}, u32[]{:S(2)}) copy-start(bf16[128,512]{1,0:T(8,128)(2,1)S(1)} %collective-permute-done.5) | copy-start | bytes 393220
  56.0 42.2 %copy-start.13 = (bf16[32,2048]{1,0:T(8,128)(2,1)}, bf16[32,2048]{1,0:T(8,128)(2,1)S(1)}, u32[]{:S(2)}) copy-start(bf16[32,2048]{1,0:T(8,128)(2,1)S(1)} %collective-permute-done) | copy-start | bytes 393220
  77.8 20.4 %copy-start.14 = (bf16[32,2048]{1,0:T(8,128)(2,1)}, bf16[32,2048]{1,0:T(8,128)(2,1)S(1)}, u32[]{:S(2)}) copy-start(bf16[32,2048]{1,0:T(8,128)(2,1)S(1)} %collective-permute-done.1) | copy-start | bytes 393220
  77.9 10.1 %copy-start.17 = (bf16[128,512]{1,0:T(8,128)(2,1)S(1)}, bf16[128,512]{1,0:T(8,128)(2,1)}, u32[]{:S(2)}) copy-start(bf16[128,512]{1,0:T(8,128)(2,1)} %copy-done.16) | copy-start | bytes 393220
  79.2 51.5 %collective-permute-start.10 = (bf16[512,1024]{1,0:T(8,128)(2,1)S(1)}, bf16[512,1024]{1,0:T(8,128)(2,1)S(1)}, u32[]{:S(2)}, u32[]{:S(2)}) collective-permute-start(bf16[512,1024]{1,0:T(8,128)(2,1)S(1)} %slice.60.refs_2_), channel_id=1, source_target_pairs={{0,128},{128,256},{256,384},{384,0},{1,129},{129,257},{257,385},{3... | collective-permute-start | bytes 3145736 | tf_op jit(solution)/shard_map/ppermute | solution.py:36
  84.0 41.6 %collective-permute-start.9 = (bf16[512,1024]{1,0:T(8,128)(2,1)S(1)}, bf16[512,1024]{1,0:T(8,128)(2,1)S(1)}, u32[]{:S(2)}, u32[]{:S(2)}) collective-permute-start(bf16[512,1024]{1,0:T(8,128)(2,1)S(1)} %slice.60.refs_2_), channel_id=1, source_target_pairs={{0,384},{128,0},{256,128},{384,256},{1,385},{129,1},{257,129},{385... | collective-permute-start | bytes 3145736 | tf_op jit(solution)/shard_map/ppermute | solution.py:36
  93.9 26.6 %all-to-all-start.1 = ((f32[4,128,512]{2,1,0:T(8,128)}), f32[4,128,512]{2,1,0:T(8,128)}, u32[]{:S(2)}, u32[]{:S(2)}) async-start(f32[4,128,512]{2,1,0:T(8,128)} %fusion.3), calls=%async_computation.1 | async-start | bytes 2097152 | tf_op jit(solution)/shard_map/all_to_all | solution.py:25
  99.3 11.1 %collective-permute-start.6 = (bf16[3,32,2048]{2,1,0:T(8,128)(2,1)S(1)}, bf16[3,32,2048]{2,1,0:T(8,128)(2,1)}, u32[]{:S(2)}, u32[]{:S(2)}) collective-permute-start(bf16[3,32,2048]{2,1,0:T(8,128)(2,1)S(1)} %pad_maximum_fusion.2.own_ref), channel_id=1, source_target_pairs={{0,2},{2,0},{1,3},{3,1},{4,6},{6,4},{5,7},{7,5},{8,10},{10,8},{9,1... | collective-permute-start | bytes 1179656 | tf_op jit(solution)/shard_map/ppermute | solution.py:36
  101.2 21.3 %collective-permute-start.7 = (bf16[3,32,2048]{2,1,0:T(8,128)(2,1)S(1)}, bf16[3,32,2048]{2,1,0:T(8,128)(2,1)}, u32[]{:S(2)}, u32[]{:S(2)}) collective-permute-start(bf16[3,32,2048]{2,1,0:T(8,128)(2,1)S(1)} %pad_maximum_fusion.2.own_ref), channel_id=1, source_target_pairs={{0,1},{1,0},{2,3},{3,2},{4,5},{5,4},{6,7},{7,6},{8,9},{9,8},{10,11... | collective-permute-start | bytes 1179656 | tf_op jit(solution)/shard_map/ppermute | solution.py:36
  110.4 12.1 %collective-permute-start.8 = (bf16[3,32,2048]{2,1,0:T(8,128)(2,1)}, bf16[3,32,2048]{2,1,0:T(8,128)(2,1)}, u32[]{:S(2)}, u32[]{:S(2)}) collective-permute-start(bf16[3,32,2048]{2,1,0:T(8,128)(2,1)} %collective-permute-done.6.near_ref), channel_id=1, source_target_pairs={{0,1},{1,0},{2,3},{3,2},{4,5},{5,4},{6,7},{7,6},{8,9},{9,8},{10,11... | collective-permute-start | bytes 1179656 | tf_op jit(solution)/shard_map/ppermute | solution.py:36
  125.6 14.2 %collective-permute-start.11 = (bf16[256,1024]{1,0:T(8,128)(2,1)S(1)}, bf16[256,1024]{1,0:T(8,128)(2,1)S(1)}, u32[]{:S(2)}, u32[]{:S(2)}) collective-permute-start(bf16[256,1024]{1,0:T(8,128)(2,1)S(1)} %slice.79), channel_id=1, source_target_pairs={{0,384},{128,0},{256,128},{384,256},{1,385},{129,1},{257,129},{385... | collective-permute-start | bytes 1572872 | tf_op jit(solution)/shard_map/ppermute | solution.py:36
  130.7 13.8 %collective-permute-start.12 = (bf16[256,1024]{1,0:T(8,128)(2,1)S(1)}, bf16[256,1024]{1,0:T(8,128)(2,1)S(1)}, u32[]{:S(2)}, u32[]{:S(2)}) collective-permute-start(bf16[256,1024]{1,0:T(8,128)(2,1)S(1)} %slice.81), channel_id=1, source_target_pairs={{0,128},{128,256},{256,384},{384,0},{1,129},{129,257},{257,385},{3... | collective-permute-start | bytes 1572872 | tf_op jit(solution)/shard_map/ppermute | solution.py:36
  151.9 15.7 %collective-permute-start.13 = (bf16[256,2048]{1,0:T(8,128)(2,1)}, bf16[256,2048]{1,0:T(8,128)(2,1)}, u32[]{:S(2)}, u32[]{:S(2)}) collective-permute-start(bf16[256,2048]{1,0:T(8,128)(2,1)} %shard_map.97), channel_id=1, source_target_pairs={{0,1},{1,0},{2,3},{3,2},{4,5},{5,4},{6,7},{7,6},{8,9},{9,8},{10,11... | collective-permute-start | bytes 3145736 | tf_op jit(solution)/shard_map/ppermute | solution.py:36
  158.3 13.8 %all-to-all-start.2 = ((bf16[4,128,512]{2,1,0:T(8,128)(2,1)}), bf16[4,128,512]{2,1,0:T(8,128)(2,1)}, u32[]{:S(2)}, u32[]{:S(2)}) async-start(bf16[4,128,512]{2,1,0:T(8,128)(2,1)} %broadcast_in_dim.37), calls=%async_computation.2 | async-start | bytes 1048576 | tf_op jit(solution)/shard_map/all_to_all | solution.py:25
  172.2 14.5 %collective-permute-start.14 = (bf16[4,32,2048]{2,1,0:T(8,128)(2,1)S(1)}, bf16[4,32,2048]{2,1,0:T(8,128)(2,1)S(1)}, u32[]{:S(2)}, u32[]{:S(2)}) collective-permute-start(bf16[4,32,2048]{2,1,0:T(8,128)(2,1)S(1)} %dynamic-slice_bitcast_fusion), channel_id=1, source_target_pairs={{0,2},{2,0},{1,3},{3,1},{4,6},{6,4},{5,7},{7,5},{8,10},{10,8},{9,1... | collective-permute-start | bytes 1572872 | tf_op jit(solution)/shard_map/ppermute | solution.py:36
  186.9 18.8 %collective-permute-start.15 = (bf16[32,2048]{1,0:T(8,128)(2,1)S(1)}, bf16[32,2048]{1,0:T(8,128)(2,1)S(1)}, u32[]{:S(2)}, u32[]{:S(2)}) collective-permute-start(bf16[32,2048]{1,0:T(8,128)(2,1)S(1)} %get-tuple-element.35), channel_id=1, source_target_pairs={{0,4},{4,8},{8,12},{12,16},{16,20},{20,24},{24,28},{28,32},{32,36}... | collective-permute-start | bytes 393224 | tf_op jit(solution)/shard_map/ppermute | solution.py:36
  188.8 16.9 %collective-permute-start.16 = (bf16[32,2048]{1,0:T(8,128)(2,1)S(1)}, bf16[32,2048]{1,0:T(8,128)(2,1)S(1)}, u32[]{:S(2)}, u32[]{:S(2)}) collective-permute-start(bf16[32,2048]{1,0:T(8,128)(2,1)S(1)} %get-tuple-element.34), channel_id=1, source_target_pairs={{0,8},{4,12},{8,16},{12,20},{16,24},{20,28},{24,32},{28,36},{32,40... | collective-permute-start | bytes 393224 | tf_op jit(solution)/shard_map/ppermute | solution.py:36
  190.7 18.5 %collective-permute-start.17 = (bf16[32,2048]{1,0:T(8,128)(2,1)S(1)}, bf16[32,2048]{1,0:T(8,128)(2,1)S(1)}, u32[]{:S(2)}, u32[]{:S(2)}) collective-permute-start(bf16[32,2048]{1,0:T(8,128)(2,1)S(1)} %get-tuple-element.33), channel_id=1, source_target_pairs={{0,12},{4,16},{8,20},{12,24},{16,28},{20,32},{24,36},{28,40},{32,4... | collective-permute-start | bytes 393224 | tf_op jit(solution)/shard_map/ppermute | solution.py:36
  195.0 37.1 %all-to-all-start.3 = ((bf16[32,16,512]{2,1,0:T(8,128)(2,1)}), bf16[32,16,512]{2,1,0:T(8,128)(2,1)S(1)}, u32[]{:S(2)}, u32[]{:S(2)}) async-start(bf16[32,16,512]{2,1,0:T(8,128)(2,1)} %bitcast.32), calls=%async_computation.3 | async-start | bytes 1048576 | tf_op jit(solution)/shard_map/all_to_all | solution.py:25
  209.3 17.4 %collective-permute-start.18 = (bf16[4,32,2048]{2,1,0:T(8,128)(2,1)S(1)}, bf16[4,32,2048]{2,1,0:T(8,128)(2,1)S(1)}, u32[]{:S(2)}, u32[]{:S(2)}) collective-permute-start(bf16[4,32,2048]{2,1,0:T(8,128)(2,1)S(1)} %pad_maximum_fusion.1.refs_0_), channel_id=1, source_target_pairs={{0,2},{2,0},{1,3},{3,1},{4,6},{6,4},{5,7},{7,5},{8,10},{10,8},{9,1... | collective-permute-start | bytes 1572872 | tf_op jit(solution)/shard_map/ppermute | solution.py:36
  211.5 21.4 %collective-permute-start.19 = (bf16[4,32,2048]{2,1,0:T(8,128)(2,1)S(1)}, bf16[4,32,2048]{2,1,0:T(8,128)(2,1)S(1)}, u32[]{:S(2)}, u32[]{:S(2)}) collective-permute-start(bf16[4,32,2048]{2,1,0:T(8,128)(2,1)S(1)} %pad_maximum_fusion.1.refs_0_), channel_id=1, source_target_pairs={{0,1},{1,0},{2,3},{3,2},{4,5},{5,4},{6,7},{7,6},{8,9},{9,8},{10,11... | collective-permute-start | bytes 1572872 | tf_op jit(solution)/shard_map/ppermute | solution.py:36
  226.8 6.8 %collective-permute-start.20 = (bf16[4,32,2048]{2,1,0:T(8,128)(2,1)S(1)}, bf16[4,32,2048]{2,1,0:T(8,128)(2,1)S(1)}, u32[]{:S(2)}, u32[]{:S(2)}) collective-permute-start(bf16[4,32,2048]{2,1,0:T(8,128)(2,1)S(1)} %collective-permute-done.18.refs_1_), channel_id=1, source_target_pairs={{0,1},{1,0},{2,3},{3,2},{4,5},{5,4},{6,7},{7,6},{8,9},{9,8},{10,11... | collective-permute-start | bytes 1572872 | tf_op jit(solution)/shard_map/ppermute | solution.py:36
  (16 other events, 55.8 us)
